TPU v7x, 32 devices: a whole 2x2x4 slice. The times are simulated.
32 devices in a mesh: dp: 8 (over y, x, core), fsdp: 4 (over z).
Axes of the slice: x: 2, y: 2, z: 4, core: 2. Of those that a mesh axis runs over, the one named last changes fastest.
Arguments:
- grad_partial: bfloat16 [8, 1, 1024, 4096], P('dp', None, 'fsdp'), may hold values from -0.375 to 0.375
- factors: float32 [8, 1024, 1024], P('dp', 'fsdp'), may hold values from -1 to 11, as said below
- bases: float32 [8, 1024, 1024], P('dp', 'fsdp'), may hold values from -1 to 2, as said below
- first_moment: float32 [8, 1024, 512], P('dp', 'fsdp'), may hold values from -0.3125 to 0.3125
- second_moment: float32 [8, 1024, 512], P('dp', 'fsdp'), may hold values from 0.003 to 0.03
Outputs:
- new_factors: float32 [8, 1024, 1024], P('dp', 'fsdp')
- new_bases: bfloat16 [8, 1024, 1024], P('dp', 'fsdp')
- new_first: float32 [8, 1024, 512], P('dp', 'fsdp')
- new_second: float32 [8, 1024, 512], P('dp', 'fsdp')
- direction: bfloat16 [8, 1024, 512], P('dp', 'fsdp')
Inputs may be any that keep to these rules, and one draw needn't show every extreme that they name: Each factors[t] is symmetric and positive definite. Each bases[t] is nonsingular.
All inputs are finite; a program needn't handle non-finite values.
Results may differ from a plain program's by a relative error of at most 0.024.
Values may be sent and summed in bfloat16 or wider, within the bound.
No kernel may reach another device: no remote copies, remote signals or barrier semaphores. Data moves between devices by JAX's collectives and lax.ppermute only.
A program may use at most 64 MiB of HBM per device.

v0:
```python
import jax
import jax.numpy as jnp
from jax import lax
from jax.sharding import PartitionSpec as P


def swapped(block, axis, distance):
    count = lax.axis_size(axis)
    route = []
    for low in range(count):
        high = low | 1 << distance
        if high != low and high < count:
            route += [(low, high), (high, low)]
    return lax.ppermute(block, axis, route)


def ordered_halves(own_half, partner_half, side_bit):
    return jnp.where(
        side_bit == 0,
        jnp.concatenate([own_half, partner_half], axis=1),
        jnp.concatenate([partner_half, own_half], axis=1),
    )


def body(grad_partial, factors, bases, first_moment, second_moment):
    row_count = factors.shape[1]
    block_width = factors.shape[2]
    half_width = block_width // 2
    side_bit = lax.axis_index("dp") % 2
    row_start = lax.axis_index("fsdp") * row_count
    partial_rows = grad_partial[0]
    row_blocks = partial_rows.shape[0]
    column_blocks = partial_rows.shape[2] // block_width
    summand = partial_rows.reshape(row_blocks, row_count, column_blocks, 2, half_width).transpose(
        0, 2, 3, 1, 4
    )
    summand = summand.reshape(-1, half_width).astype(jnp.float32)
    grad_half = lax.psum_scatter(
        summand.astype(jnp.bfloat16), "dp", scatter_dimension=0, tiled=True
    )
    partner_half = swapped(grad_half, "dp", 0)
    own_rows = ordered_halves(grad_half, partner_half, side_bit)
    whole_block = lax.all_gather(own_rows, "fsdp", axis=0, tiled=True)

    def left_term():
        return lax.dot_general(
            own_rows, whole_block, (((1,), (1,)), ((), ())), preferred_element_type=jnp.float32
        )

    def right_term():
        column_rows = lax.dynamic_slice_in_dim(whole_block, row_start, row_count, 1)
        return lax.dot_general(
            column_rows, whole_block, (((0,), (0,)), ((), ())), preferred_element_type=jnp.float32
        )

    outer_term = lax.cond(side_bit == 0, left_term, right_term)
    new_factor = 0.95 * factors[0] + 0.05 * outer_term
    columns = new_factor
    power_rows = jnp.dot(
        columns,
        lax.all_gather(bases[0], "fsdp", axis=0, tiled=True),
        precision=lax.Precision.HIGHEST,
        preferred_element_type=jnp.float32,
    )
    power_whole = lax.all_gather(power_rows, "fsdp", axis=0, tiled=True)
    gram_matrix = lax.dot_general(
        power_whole,
        power_whole,
        (((0,), (0,)), ((), ())),
        precision=lax.Precision.HIGHEST,
        preferred_element_type=jnp.float32,
    )
    cholesky_factor = jnp.linalg.cholesky(gram_matrix)
    new_rows = lax.linalg.triangular_solve(
        cholesky_factor, power_rows, left_side=False, lower=True, transpose_a=True
    ).astype(jnp.bfloat16)
    partner_rows = swapped(new_rows, "dp", 0)
    left_rows = jnp.where(side_bit == 0, new_rows, partner_rows)
    right_rows = jnp.where(side_bit == 0, partner_rows, new_rows)
    left_full, right_full = (
        lax.all_gather(left_rows, "fsdp", axis=0, tiled=True),
        lax.all_gather(right_rows, "fsdp", axis=0, tiled=True),
    )
    left_columns = lax.dynamic_slice_in_dim(left_full, row_start, row_count, 1)
    mixed_rows = lax.dot_general(
        left_columns, whole_block, (((0,), (0,)), ((), ())), preferred_element_type=jnp.float32
    ).astype(jnp.bfloat16)
    right_half = lax.dynamic_slice_in_dim(right_full, side_bit * half_width, half_width, 1)
    rotated = jnp.dot(mixed_rows, right_half, preferred_element_type=jnp.float32)
    first_new = 0.95 * first_moment[0] + 0.05 * rotated
    second_new = 0.95 * second_moment[0] + 0.05 * rotated * rotated
    normalized = (first_new / (jnp.sqrt(second_new) + 1e-08)).astype(jnp.bfloat16)
    columns = left_rows
    weighted_half = jnp.dot(
        columns,
        lax.all_gather(normalized, "fsdp", axis=0, tiled=True),
        preferred_element_type=jnp.float32,
    ).astype(jnp.bfloat16)
    weighted_other = swapped(weighted_half, "dp", 0)
    weighted_rows = ordered_halves(weighted_half, weighted_other, side_bit)
    right_slice = lax.dynamic_slice_in_dim(right_full, side_bit * half_width, half_width, 0)
    combined = lax.dot_general(
        weighted_rows, right_slice, (((1,), (1,)), ((), ())), preferred_element_type=jnp.float32
    ).astype(jnp.bfloat16)
    return (new_factor[None], new_rows[None], first_new[None], second_new[None], combined[None])


def solution(mesh):
    return jax.shard_map(
        body,
        mesh=mesh,
        in_specs=(
            P("dp", None, "fsdp", None),
            P("dp", "fsdp", None),
            P("dp", "fsdp", None),
            P("dp", "fsdp", None),
            P("dp", "fsdp", None),
        ),
        out_specs=(
            P("dp", "fsdp", None),
            P("dp", "fsdp", None),
            P("dp", "fsdp", None),
            P("dp", "fsdp", None),
            P("dp", "fsdp", None),
        ),
        check_vma=False,
    )
```

profile of v0, /device:TPU:13, one launch (start us, length us, event | category | flops | bytes accessed | tf_op | source)
XLA Modules:
  0.0 789.1 jit_solution(14052768063125340025)
XLA Ops:
  23.6 42.4 %reduce-scatter.2.cloned.1.call-done = bf16[256,512]{0,1:T(8,128)(2,1)} async-done(((bf16[2048,512]{0,1:T(8,128)(2,1)}), bf16[256,512]{0,1:T(8,128)(2,1)}) %reduce-scatter.2.cloned.1.call-update) | async-done | bytes 262160 | tf_op jit(solution)/shard_map/reduce_scatter | solution.py:38
  70.9 42.6 %all-gather.8.cloned.1.call-done = bf16[1024,1024]{0,1:T(8,128)(2,1)} async-done(((bf16[256,1024]{0,1:T(8,128)(2,1)}), bf16[1024,1024]{0,1:T(8,128)(2,1)}) %all-gather.8.cloned.1.call-update) | async-done | bytes 2097168 | tf_op jit(solution)/shard_map/all_gather | solution.py:43
  119.8 74.7 %all-gather.18.cloned.1.call-done = f32[1,1024,1024]{2,1,0:T(8,128)} async-done(((f32[1,256,1024]{2,1,0:T(8,128)}), f32[1,1024,1024]{2,1,0:T(8,128)}) %all-gather.18.cloned.1.call-update) | async-done | bytes 4194320 | tf_op jit(solution)/shard_map/all_gather | solution.py:61
  202.0 79.2 %all-gather.10.cloned.1.call-done = f32[1024,1024]{1,0:T(8,128)} async-done(((f32[256,1024]{1,0:T(8,128)}), f32[1024,1024]{1,0:T(8,128)}) %all-gather.10.cloned.1.call-update) | async-done | bytes 4194320 | tf_op jit(solution)/shard_map/all_gather | solution.py:65
  281.2 17.6 %fusion.94 = f32[1024,1024]{1,0:T(8,128)} fusion(f32[1024,1024]{1,0:T(8,128)} %all-gather.10.cloned.1.call-done), kind=kOutput, calls=%fused_computation.201 | convolution fusion | flops 12884901888 | bytes 8388608 | tf_op jit(solution)/shard_map/dot_general | solution.py:66
  310.9 11.7 %cholesky.223 = f32[128,128]{1,0:T(8,128)S(1)} custom-call(f32[128,128]{1,0:T(8,128)S(1)} %cholesky.580), custom_call_target="Cholesky" | custom-call | tf_op jit(solution)/shard_map/jit(cholesky)/cholesky | solution.py:73
  325.2 9.8 %custom-call.62 = f32[1,128,128]{1,2,0:T(8,128)S(1)} custom-call(f32[1,128,128]{2,1,0:T(8,128)S(1)} %get-tuple-element.90), custom_call_target="InvertDiagBlocksLowerTriangular" | custom-call | tf_op jit(solution)/shard_map/jit(cholesky)/cholesky | solution.py:73
  338.9 11.9 %cholesky.244 = f32[128,128]{1,0:T(8,128)S(1)} custom-call(f32[128,128]{1,0:T(8,128)S(1)} %cholesky.584), custom_call_target="Cholesky" | custom-call | tf_op jit(solution)/shard_map/jit(cholesky)/cholesky | solution.py:73
  351.4 9.8 %custom-call.63 = f32[1,128,128]{1,2,0:T(8,128)S(1)} custom-call(f32[1,128,128]{2,1,0:T(8,128)S(1)} %get-tuple-element.87), custom_call_target="InvertDiagBlocksLowerTriangular" | custom-call | tf_op jit(solution)/shard_map/jit(cholesky)/cholesky | solution.py:73
  364.6 11.7 %cholesky.468 = f32[128,128]{1,0:T(8,128)S(1)} custom-call(f32[128,128]{1,0:T(8,128)S(1)} %cholesky.589), custom_call_target="Cholesky" | custom-call | tf_op jit(solution)/shard_map/jit(cholesky)/cholesky | solution.py:73
  377.6 9.8 %custom-call.64 = f32[1,128,128]{1,2,0:T(8,128)S(1)} custom-call(f32[1,128,128]{2,1,0:T(8,128)S(1)} %get-tuple-element.84), custom_call_target="InvertDiagBlocksLowerTriangular" | custom-call | tf_op jit(solution)/shard_map/jit(cholesky)/cholesky | solution.py:73
  390.9 11.9 %cholesky.487 = f32[128,128]{1,0:T(8,128)S(1)} custom-call(f32[128,128]{1,0:T(8,128)S(1)} %cholesky.594), custom_call_target="Cholesky" | custom-call | tf_op jit(solution)/shard_map/jit(cholesky)/cholesky | solution.py:73
  404.1 9.8 %custom-call.65 = f32[1,128,128]{1,2,0:T(8,128)S(1)} custom-call(f32[1,128,128]{2,1,0:T(8,128)S(1)} %get-tuple-element.81), custom_call_target="InvertDiagBlocksLowerTriangular" | custom-call | tf_op jit(solution)/shard_map/jit(cholesky)/cholesky | solution.py:73
  417.4 11.7 %cholesky.506 = f32[128,128]{1,0:T(8,128)S(1)} custom-call(f32[128,128]{1,0:T(8,128)S(1)} %cholesky.599), custom_call_target="Cholesky" | custom-call | tf_op jit(solution)/shard_map/jit(cholesky)/cholesky | solution.py:73
  430.4 10.2 %custom-call.66 = f32[1,128,128]{1,2,0:T(8,128)S(1)} custom-call(f32[1,128,128]{2,1,0:T(8,128)S(1)} %get-tuple-element.78), custom_call_target="InvertDiagBlocksLowerTriangular" | custom-call | tf_op jit(solution)/shard_map/jit(cholesky)/cholesky | solution.py:73
  443.9 11.7 %cholesky.526 = f32[128,128]{1,0:T(8,128)S(1)} custom-call(f32[128,128]{1,0:T(8,128)S(1)} %cholesky.604), custom_call_target="Cholesky" | custom-call | tf_op jit(solution)/shard_map/jit(cholesky)/cholesky | solution.py:73
  456.9 9.8 %custom-call.67 = f32[1,128,128]{1,2,0:T(8,128)S(1)} custom-call(f32[1,128,128]{2,1,0:T(8,128)S(1)} %get-tuple-element.75), custom_call_target="InvertDiagBlocksLowerTriangular" | custom-call | tf_op jit(solution)/shard_map/jit(cholesky)/cholesky | solution.py:73
  469.7 11.9 %cholesky.546 = f32[128,128]{1,0:T(8,128)S(1)} custom-call(f32[128,128]{1,0:T(8,128)S(1)} %cholesky.609), custom_call_target="Cholesky" | custom-call | tf_op jit(solution)/shard_map/jit(cholesky)/cholesky | solution.py:73
  495.4 11.7 %cholesky.564 = f32[128,128]{1,0:T(8,128)S(1)} custom-call(f32[128,128]{1,0:T(8,128)S(1)} %convolution_subtract_fusion.13), custom_call_target="Cholesky" | custom-call | tf_op jit(solution)/shard_map/jit(cholesky)/cholesky | solution.py:73
  518.9 27.6 %while.1 = (s32[]{:T(128)}, f32[1024,1024]{1,0:T(8,128)}, s32[8,2]{0,1:T(2,128)S(1)}, f32[8,128,128]{2,1,0:T(8,128)}, s32[]{:T(128)}) while((s32[]{:T(128)}, f32[1024,1024]{1,0:T(8,128)}, s32[8,2]{0,1:T(2,128)S(1)}, f32[8,128,128]{2,1,0:T(8,128)}, s32[]{:T(128)}) %tuple.72), condition=%wide.while_cond, body=%wide.while_body.sunk | while | flops 2 | bytes 132705 | solution.py:74
  546.5 79.6 %custom-call.69 = f32[8,128,128]{1,2,0:T(8,128)S(1)} custom-call(f32[8,128,128]{2,1,0:T(8,128)} %get-tuple-element.27), custom_call_target="InvertDiagBlocksLowerTriangular" | custom-call | tf_op jit(solution)/shard_map/triangular_solve | solution.py:74
  650.3 43.7 %all-gather.12.cloned.1.call-done = bf16[1024,1024]{0,1:T(8,128)(2,1)} async-done(((bf16[256,1024]{0,1:T(8,128)(2,1)}), bf16[1024,1024]{0,1:T(8,128)(2,1)}) %all-gather.12.cloned.1.call-update) | async-done | bytes 2097168 | tf_op jit(solution)/shard_map/all_gather | solution.py:81
  694.0 46.6 %all-gather.14.cloned.1.call-done = bf16[1024,1024]{0,1:T(8,128)(2,1)} async-done(((bf16[256,1024]{0,1:T(8,128)(2,1)}), bf16[1024,1024]{0,1:T(8,128)(2,1)}) %all-gather.14.cloned.1.call-update) | async-done | bytes 2097168 | tf_op jit(solution)/shard_map/all_gather | solution.py:82
  744.6 28.8 %all-gather.16.cloned.1.call-done = bf16[1024,512]{1,0:T(8,128)(2,1)} async-done(((bf16[256,512]{1,0:T(8,128)(2,1)}), bf16[1024,512]{1,0:T(8,128)(2,1)}) %all-gather.16.cloned.1.call-update) | async-done | bytes 1048592 | tf_op jit(solution)/shard_map/all_gather | solution.py:96
  (146 shorter events, 167.0 us)
Async XLA Ops:
  7.2 58.9 %reduce-scatter.2.cloned.1.call-start = ((), (), s32[]{:S(2)}) async-start(), calls=%async_computation.1 | async-start | bytes 2359296 | tf_op jit(solution)/shard_map/reduce_scatter | solution.py:38
  23.6 90.0 %all-gather.8.cloned.1.call-start = ((), (), s32[]{:S(2)}) async-start(), calls=%async_computation.2 | async-start | bytes 2621440 | tf_op jit(solution)/shard_map/all_gather | solution.py:43
  66.0 2.0 collective-permute-start
  70.1 124.4 %all-gather.18.cloned.1.call-start = ((), (), s32[]{:S(2)}) async-start(), calls=%async_computation.7 | async-start | bytes 5242880 | tf_op jit(solution)/shard_map/all_gather | solution.py:61
  70.9 210.3 %all-gather.10.cloned.1.call-start = ((), (), s32[]{:S(2)}) async-start(), calls=%async_computation.3 | async-start | bytes 5242880 | tf_op jit(solution)/shard_map/all_gather | solution.py:65
  113.6 4.1 copy-start.1
  201.7 492.3 %all-gather.12.cloned.1.call-start = ((), (), s32[]{:S(2)}) async-start(), calls=%async_computation.4 | async-start | bytes 2621440 | tf_op jit(solution)/shard_map/all_gather | solution.py:81
  309.0 2.0 copy-start.2
  514.0 112.1 %copy-start.3 = (f32[256,1024]{1,0:T(8,128)S(1)}, f32[256,1024]{1,0:T(8,128)}, u32[]{:S(2)}) copy-start(f32[256,1024]{1,0:T(8,128)} %fusion.4) | copy-start | bytes 3145732
  626.1 8.3 %copy-start.6 = (f32[8,128,128]{1,2,0:T(8,128)}, f32[8,128,128]{1,2,0:T(8,128)S(1)}, u32[]{:S(2)}) copy-start(f32[8,128,128]{1,2,0:T(8,128)S(1)} %custom-call.69) | copy-start | bytes 1572868
  636.7 103.9 %copy-start = (bf16[1024,1024]{0,1:T(8,128)(2,1)S(1)}, bf16[1024,1024]{0,1:T(8,128)(2,1)}, u32[]{:S(2)}) copy-start(bf16[1024,1024]{0,1:T(8,128)(2,1)} %all-gather.8.cloned.1.call-done) | copy-start | bytes 6291460
  645.6 0.8 copy-start.4
  646.4 2.2 collective-permute-start.1
  649.7 90.9 %all-gather.14.cloned.1.call-start = ((), (), s32[]{:S(2)}) async-start(), calls=%async_computation.5 | async-start | bytes 2621440 | tf_op jit(solution)/shard_map/all_gather | solution.py:82
  650.3 123.1 %all-gather.16.cloned.1.call-start = ((), (), s32[]{:S(2)}) async-start(), calls=%async_computation.6 | async-start | bytes 1310720 | tf_op jit(solution)/shard_map/all_gather | solution.py:96
  744.6 34.1 %copy-start.5 = (bf16[1,256,1024]{1,2,0:T(8,128)(2,1)S(1)}, bf16[1,256,1024]{1,2,0:T(8,128)(2,1)}, u32[]{:S(2)}) copy-start(bf16[1,256,1024]{1,2,0:T(8,128)(2,1)} %copy-done.4) | copy-start | bytes 1572868
  775.3 4.4 collective-permute-start.2
Sparse Core Ops, SparseCore 0:
  23.7 42.2 reduce-scatter.1
  70.2 43.2 all-gather.7
  115.2 79.2 all-gather.17
  201.8 79.2 all-gather.9
  649.8 44.1 all-gather.11
  696.1 44.4 all-gather.13
  744.7 28.5 all-gather.15
where the time goes:
time: 797 us; the launch traced here: 789 us
  waiting for transfers between devices  362 us (45%)
  other arithmetic  267 us (34%)
  matrix products  77.4 us (10%)
  local copies, waits for them, and re-layouts  60.2 us (8%)
  between operations  19.8 us (2%)
    another operation x30, other arithmetic, body(): cholesky_factor = jnp.linalg.cholesky(gram_matrix)  172 us
    another operation x3, other arithmetic, body(): lax.linalg.triangular_solve(cholesky_factor, power_rows, left_side=False,...  84.5 us
    all_gather x1, waiting for transfers between devices, body(): power_whole = lax.all_gather(power_rows, 'fsdp', axis=0, tiled=True)  79.2 us
    all_gather x1, waiting for transfers between devices, body(): lax.all_gather(bases[0], 'fsdp', axis=0, tiled=True)  74.7 us
    all_gather x1, waiting for transfers between devices, body(): lax.all_gather(right_rows, 'fsdp', axis=0, tiled=True)  46.6 us
    all_gather x1, waiting for transfers between devices, body(): lax.all_gather(left_rows, 'fsdp', axis=0, tiled=True)  43.7 us
    all_gather x1, waiting for transfers between devices, body(): whole_block = lax.all_gather(own_rows, 'fsdp', axis=0, tiled=True)  42.6 us
    reduce_scatter x1, waiting for transfers between devices, body(): lax.psum_scatter(summand.astype(jnp.bfloat16), 'dp', scatter_dimension=0,...  42.4 us
  transfers between devices with their start and end apart: 10, of which 9 were waited for; matrix products, arithmetic and copies ran while one was open for 1% of the time, Pallas kernels for 0%

commit v1 on v0

v1 whole, which is shorter than its diff:
```python
import functools

import jax
import jax.numpy as jnp
from jax import lax
from jax.experimental import pallas as pl
from jax.experimental.pallas import tpu as pltpu
from jax.sharding import PartitionSpec as P

TILE = 128
SUB = 8
VMEM_GRANT = 60 * 2**20


def splat_lane(x, lane):
    return jnp.broadcast_to(x[:, lane : lane + 1], x.shape)


def splat_row(x, row):
    return jnp.broadcast_to(x[row : row + 1, :], x.shape)


def reciprocal(x):
    guess = pl.reciprocal(x, approx=True)
    return guess * (2.0 - x * guess)


def tree_sum(terms):
    while len(terms) > 1:
        terms = [x + y for x, y in zip(terms[0::2], terms[1::2])]
    return terms[0]


def inverse_columns(columns, sub):
    held = list(columns)
    for p in range(0, SUB, 2):
        first, second = held[p], held[p + 1]
        a, b, c = splat_row(first, p), splat_row(second, p), splat_row(second, p + 1)
        det = reciprocal(a * c - b * b)
        ia, ib, ic = c * det, -b * det, a * det
        at_first, at_second = sub == p, sub == p + 1
        for k in range(SUB):
            if k == p:
                s, t = ia, ib
                kept = jnp.zeros_like(first)
            elif k == p + 1:
                s, t = ib, ic
                kept = jnp.zeros_like(first)
            else:
                u, v = splat_row(held[k], p), splat_row(held[k], p + 1)
                s, t = ia * u + ib * v, ib * u + ic * v
                kept = held[k]
            rest = kept - (first * s + second * t)
            held[k] = jnp.where(at_first, s, jnp.where(at_second, t, rest))
    return held


def scaled_rows(columns, rows, sub):
    columns = list(columns)
    for p in range(SUB):
        pivot = splat_row(columns[p], p)
        scale = lax.rsqrt(pivot)
        factor = jnp.where(sub > p, columns[p] * (scale * scale), 0.0)
        for k in range(p + 1, SUB):
            columns[k] = columns[k] - factor * splat_row(columns[k], p)
        rows = jnp.where(sub == p, rows * scale, rows - factor * splat_row(rows, p))
    return rows


def tile_inverse(tile):
    size = tile.shape[0]
    count = size // SUB
    lane = lax.broadcasted_iota(jnp.int32, (SUB, size), 1)
    sub = lax.broadcasted_iota(jnp.int32, (SUB, size), 0)
    groups = [tile[SUB * g : SUB * (g + 1), :] for g in range(count)]
    result = []
    for g in range(count):
        base = SUB * g
        in_block = (lane >= base) & (lane < base + SUB)
        pivots = [splat_lane(groups[g], base + k) for k in range(SUB)]
        inverse = inverse_columns(pivots, sub)
        one = jnp.where(lane == base + sub, 1.0, 0.0)
        own = jnp.where(in_block, one, groups[g])
        result.append(scaled_rows(pivots, jnp.where(lane < base, groups[g], one), sub))
        if g == count - 1:
            break
        applied = tree_sum([inverse[k] * splat_row(own, k) for k in range(SUB)])
        spread = [splat_row(applied, k) for k in range(SUB)]
        for h in range(g + 1, count):
            taken = tree_sum([splat_lane(groups[h], base + k) * spread[k] for k in range(SUB)])
            groups[h] = jnp.where(in_block, 0.0, groups[h]) - taken
    return jnp.concatenate(result, axis=0)


def split_cat(x, which, axis):
    hi = x.astype(jnp.bfloat16)
    lo = (x - hi.astype(jnp.float32)).astype(jnp.bfloat16)
    return jnp.concatenate([hi if w == "h" else lo for w in which], axis=axis)


def product(x, y, dims):
    return lax.dot_general(x, y, (dims, ((), ())), preferred_element_type=jnp.float32)


def product3(x, y, dims):
    (cx,), (cy,) = dims
    return product(split_cat(x, "hhl", cx), split_cat(y, "hlh", cy), dims)


NN, NT, TN = ((1,), (0,)), ((1,), (1,)), ((0,), (0,))


def invert_factor(ref):
    order = ref.shape[0]
    tiles = order // TILE
    lane = lax.broadcasted_iota(jnp.int32, (TILE, order), 1)
    row = lax.broadcasted_iota(jnp.int32, (TILE, order), 0)

    def step(j, carry):
        start = pl.multiple_of(j * TILE, TILE)
        rows = pl.ds(start, TILE)
        inverse = tile_inverse(ref[rows, rows])
        in_tile = (lane >= start) & (lane < start + TILE)
        whole = jnp.where(in_tile, jnp.where(lane - start == row, 1.0, 0.0), ref[rows, :])
        reduced = product3(inverse, whole, NN)
        ref[rows, :] = jnp.where(lane < start + TILE, reduced, 0.0)
        right = split_cat(reduced, "hlh", 0)

        def update(i, c):
            below = pl.ds(pl.multiple_of(i * TILE, TILE), TILE)
            left = product3(ref[below, rows], inverse, NT)
            kept = jnp.where(in_tile, 0.0, ref[below, :])
            ref[below, :] = kept - product(split_cat(left, "hhl", 1), right, NN)
            return c

        lax.fori_loop(j + 1, tiles, update, 0)
        return carry

    lax.fori_loop(0, tiles, step, 0)


HBM = pl.BlockSpec(memory_space=pl.ANY)
SMEM = pl.BlockSpec(memory_space=pltpu.SMEM)


def kernel_call(kernel, name, out_shape, scratch, flops, operands):
    return pl.pallas_call(
        kernel,
        out_shape=out_shape,
        in_specs=[SMEM] + [HBM] * (len(operands) - 1),
        out_specs=jax.tree.map(lambda _: HBM, out_shape),
        scratch_shapes=scratch,
        cost_estimate=pl.CostEstimate(flops=flops, bytes_accessed=16 * 2**20, transcendentals=0),
        compiler_params=pltpu.CompilerParams(vmem_limit_bytes=VMEM_GRANT),
        name=name,
    )(*operands)


class Copies:
    def __init__(self, semaphores):
        self.semaphores, self.used = semaphores, 0

    def start(self, source, target):
        copy = pltpu.make_async_copy(source, target, self.semaphores.at[self.used])
        self.used += 1
        copy.start()
        return copy

    def start_either(self, first, zero_source, one_source, target):
        semaphore = self.semaphores.at[self.used]
        self.used += 1

        @pl.when(first)
        def _():
            pltpu.make_async_copy(zero_source, target, semaphore).start()

        @pl.when(jnp.logical_not(first))
        def _():
            pltpu.make_async_copy(one_source, target, semaphore).start()

        return pltpu.make_async_copy(zero_source, target, semaphore)


def rows_from(position, distance, row_count, count):
    source = lax.rem(position - distance + count, count)
    return pl.ds(pl.multiple_of(source * row_count, row_count), row_count)


def orthonormalize(power_ref, q_ref, gram_ref):
    bf16 = jnp.bfloat16
    width = gram_ref.shape[0]
    for start in range(0, power_ref.shape[1], width):
        span = slice(start, start + width)
        group = power_ref[:, span]
        if start > 0:
            along = product(q_ref[:, :start], group.astype(bf16), TN).astype(bf16)
            group = group - product(q_ref[:, :start], along, NN)
        group = group.astype(bf16)
        gram_ref[...] = product(group, group, TN)
        invert_factor(gram_ref)
        inverse = split_cat(gram_ref[...], "hl", 1)
        q_ref[:, span] = product(jnp.concatenate([group, group], axis=1), inverse, NT).astype(bf16)


def share_kernel(symmetric, place_ref, factor_ref, basis_ref, share_ref):
    row_count, order = factor_ref.shape
    count = order // row_count
    width = order // 4
    bf16 = jnp.bfloat16
    shared = share_ref.shape[1] - width
    share_ref[:, shared:] = basis_ref[:, width : 2 * width].astype(bf16)
    if not symmetric:
        share_ref[:, :shared] = factor_ref[...].astype(bf16)
        return
    half = row_count // 2
    for r in range(count):

        @pl.when(place_ref[1] == r)
        def _():
            for offset in range(count // 2):
                start = (r + offset) % count * row_count
                share_ref[:, offset * row_count : (offset + 1) * row_count] = factor_ref[
                    :, start : start + row_count
                ].astype(bf16)
            start = (r + count // 2) % count * row_count
            if r < count // 2:
                last = factor_ref[:, start : start + half]
            else:
                last = factor_ref[half:, start : start + row_count].T
            share_ref[:, count // 2 * row_count : shared] = last.astype(bf16)


def gather_share(place, factor_rows, basis_rows, symmetric):
    row_count, order = factor_rows.shape
    shared = order // 2 + row_count // 2 if symmetric else order
    vmem = pl.BlockSpec(memory_space=pltpu.VMEM)
    return pl.pallas_call(
        functools.partial(share_kernel, symmetric),
        out_shape=jax.ShapeDtypeStruct((row_count, shared + order // 4), jnp.bfloat16),
        in_specs=[SMEM, vmem, vmem],
        out_specs=vmem,
        cost_estimate=pl.CostEstimate(flops=0, bytes_accessed=3 * 2**20, transcendentals=0),
        compiler_params=pltpu.CompilerParams(vmem_limit_bytes=VMEM_GRANT),
        name="gather_share",
    )(place, factor_rows, basis_rows)


def first_kernel(half_steps, count, place_ref, gathered_hbm, rows_hbm, *refs):
    own, other, basis = refs[:count], refs[count : 2 * count], refs[2 * count : 3 * count]
    whole_hbm, new_rows_hbm, q_hbm = refs[3 * count : 3 * count + 3]
    block, old, columns, rows, whole, new_rows, power, q, gram, semaphores = refs[3 * count + 3 :]
    row_count, order = rows.shape
    half_width = order // 2
    width = order // 4
    shared = old.shape[1]
    first = place_ref[0] == 0
    copies = Copies(semaphores)
    waits, late = [], []
    for k in range(count):
        span = rows_from(place_ref[1], k, row_count, count)
        waits.append(copies.start_either(first, own[k], other[k], block.at[span, pl.ds(0, half_width)]))
        waits.append(copies.start_either(first, other[k], own[k], block.at[span, pl.ds(half_width, half_width)]))
    waits.append(copies.start(gathered_hbm.at[:, pl.ds(0, shared)], old))
    waits.append(copies.start(rows_hbm, rows))
    late.append(copies.start(gathered_hbm.at[:, pl.ds(shared, width)], columns.at[:, pl.ds(width, width)]))
    for k in range(count):
        span = rows_from(place_ref[1], k, row_count, count)
        late.append(copies.start(basis[k], columns.at[span, pl.ds(0, width)]))
    for copy in waits:
        copy.wait()

    def old_block(r, c):
        offset = (c - r) % count
        row = slice(r * row_count, (r + 1) * row_count)
        if half_steps is None:
            return old[row, c * row_count : (c + 1) * row_count].astype(jnp.float32)
        if offset < half_steps:
            return old[row, offset * row_count : (offset + 1) * row_count].astype(jnp.float32)
        if offset > half_steps or r >= half_steps:
            return old_block(c, r).T
        mirror = slice(c * row_count, (c + 1) * row_count)
        part = slice(half_steps * row_count, half_steps * row_count + row_count // 2)
        return jnp.concatenate([old[row, part], old[mirror, part]], axis=1).astype(jnp.float32)

    @pl.when(first)
    def _():
        for start in range(0, order, width):
            power[start : start + width, :] = product(block[start : start + width, :], block[...], NT)

    @pl.when(jnp.logical_not(first))
    def _():
        for start in range(0, order, width):
            power[start : start + width, :] = product(block[:, start : start + width], block[...], TN)

    here = rows_from(place_ref[1], 0, row_count, count)
    new_rows[...] = 0.95 * rows[...] + 0.05 * power[here, :]
    for r in range(count):
        row = slice(r * row_count, (r + 1) * row_count)
        rest = jnp.concatenate([old_block(r, c) for c in range(count)], axis=1)
        whole[row, :] = (0.95 * rest + 0.05 * power[row, :]).astype(jnp.bfloat16)
    outputs = [copies.start(new_rows, new_rows_hbm), copies.start(whole, whole_hbm)]
    for copy in late:
        copy.wait()
    power[:, :half_width] = product(whole[...], columns[...], NN)
    orthonormalize(power.at[:, pl.ds(0, half_width)], q, gram)
    outputs.append(copies.start(q, q_hbm))
    for copy in outputs:
        copy.wait()


def first_half(place, own, other, basis, gathered, rows, half_steps):
    row_count, order = rows.shape
    count = len(own)
    half = order // 2
    bf16, f32 = jnp.bfloat16, jnp.float32
    shape, vmem = jax.ShapeDtypeStruct, pltpu.VMEM
    return kernel_call(
        functools.partial(first_kernel, half_steps, count),
        "first_half",
        (shape((order, order), bf16), shape(rows.shape, f32), shape((order, half), bf16)),
        [
            vmem((order, order), bf16),
            vmem((order, gathered.shape[1] - order // 4), bf16),
            vmem((order, half), bf16),
            vmem(rows.shape, f32),
            vmem((order, order), bf16),
            vmem(rows.shape, f32),
            vmem((order, order), f32),
            vmem((order, half), bf16),
            vmem((half // 2, half // 2), f32),
            pltpu.SemaphoreType.DMA((3 * count + 6,)),
        ],
        6 * order**3,
        (place, gathered, rows, *own, *other, *basis),
    )


def second_kernel(count, place_ref, whole_hbm, before_hbm, *refs):
    basis, (q_hbm, rows_hbm) = refs[:count], refs[count : count + 2]
    whole, before, columns, power, q, gram, semaphores = refs[count + 2 :]
    order, half = before.shape
    row_count = order // count
    bf16 = jnp.bfloat16
    here = rows_from(place_ref[1], 0, row_count, count)
    copies = Copies(semaphores)
    waits = [copies.start(whole_hbm, whole)]
    for k in range(count):
        waits.append(copies.start(basis[k], columns.at[rows_from(place_ref[1], k, row_count, count), :]))
    last = copies.start(before_hbm, before)
    for copy in waits:
        copy.wait()
    power[...] = product(whole[...], columns[...], NN)
    last.wait()
    outputs = [copies.start(before.at[here, :], rows_hbm.at[:, pl.ds(0, half)])]
    along = product(before[...], power[...].astype(bf16), TN)
    power[...] = power[...] - product(before[...], along.astype(bf16), NN)
    orthonormalize(power, q, gram)
    outputs.append(copies.start(q, q_hbm))
    outputs.append(copies.start(q.at[here, :], rows_hbm.at[:, pl.ds(half, half)]))
    for copy in outputs:
        copy.wait()


def second_half(place, basis, whole, before):
    order, half = before.shape
    row_count = order // len(basis)
    bf16, f32 = jnp.bfloat16, jnp.float32
    shape, vmem = jax.ShapeDtypeStruct, pltpu.VMEM
    return kernel_call(
        functools.partial(second_kernel, len(basis)),
        "second_half",
        (shape((order, half), bf16), shape((row_count, order), bf16)),
        [
            vmem((order, order), bf16),
            vmem((order, half), bf16),
            vmem((order, half), bf16),
            vmem((order, half), f32),
            vmem((order, half), bf16),
            vmem((half // 2, half // 2), f32),
            pltpu.SemaphoreType.DMA((len(basis) + 5,)),
        ],
        4 * order**3,
        (place, whole, before, *basis),
    )


def moment_kernel(count, place_ref, *refs):
    own, other, own_pieces, other_pieces = refs[:2], refs[2:4], refs[4 : 4 + count], refs[4 + count : 4 + 2 * count]
    moments_hbm, first_hbm, second_hbm = refs[4 + 2 * count : 7 + 2 * count]
    weighted_hbm, first_out, second_out = refs[7 + 2 * count : 10 + 2 * count]
    left, right, block, moments, first_rows, second_rows, mixed, rotated, normal, weighted, semaphores = refs[
        10 + 2 * count :
    ]
    row_count, half_width = first_rows.shape
    order = left.shape[0]
    f32, bf16 = jnp.float32, jnp.bfloat16
    first = place_ref[0] == 0
    here = rows_from(place_ref[1], 0, row_count, count)
    upper, lower = pl.ds(0, half_width), pl.ds(half_width, half_width)
    copies = Copies(semaphores)
    early = [copies.start_either(first, other[0], own[1], right)]
    for k in range(count):
        span = rows_from(place_ref[1], k, row_count, count)
        early.append(copies.start_either(first, own_pieces[k], other_pieces[k], block.at[span, upper]))
        early.append(copies.start_either(first, other_pieces[k], own_pieces[k], block.at[span, lower]))
    late = [
        copies.start_either(first, own[0], other[0], left.at[:, upper]),
        copies.start_either(first, own[1], other[1], left.at[:, lower]),
        copies.start(moments_hbm, moments),
        copies.start(first_hbm, first_rows),
        copies.start(second_hbm, second_rows),
    ]
    for copy in early:
        copy.wait()
    mixed[...] = product(block[...], right[...], NN).astype(bf16)
    for copy in late:
        copy.wait()
    total = jnp.zeros(weighted.shape, f32)
    width = order // 4
    for start in range(0, order, width):
        span = slice(start, start + width)
        turn = product(left[:, span], mixed[...], TN)
        rotated[span, :] = turn
        new_first = 0.95 * moments[span, :half_width].astype(f32) + 0.05 * turn
        new_second = 0.95 * moments[span, half_width:].astype(f32) + 0.05 * turn * turn
        normal[span, :] = (new_first / (jnp.sqrt(new_second) + 1e-08)).astype(bf16)
        total = total + product(left[here, span], normal[span, :], NN)
    weighted[...] = total.astype(bf16)
    outputs = [copies.start(weighted, weighted_hbm)]
    turn = rotated[here, :]
    first_rows[...] = 0.95 * first_rows[...] + 0.05 * turn
    second_rows[...] = 0.95 * second_rows[...] + 0.05 * turn * turn
    outputs += [copies.start(first_rows, first_out), copies.start(second_rows, second_out)]
    for copy in outputs:
        copy.wait()


def moment_step(place, own, other, own_pieces, other_pieces, moments, first, second):
    order = own[0].shape[0]
    half = first.shape[1]
    count = len(own_pieces)
    f32, bf16 = jnp.float32, jnp.bfloat16
    shape, vmem = jax.ShapeDtypeStruct, pltpu.VMEM
    return kernel_call(
        functools.partial(moment_kernel, count),
        "moment_step",
        (shape(first.shape, bf16), shape(first.shape, f32), shape(first.shape, f32)),
        [
            vmem((order, order), bf16),
            vmem((order, half), bf16),
            vmem((order, order), bf16),
            vmem((order, order), bf16),
            vmem(first.shape, f32),
            vmem(first.shape, f32),
            vmem((order, half), bf16),
            vmem((order, half), f32),
            vmem((order, half), bf16),
            vmem(first.shape, bf16),
            pltpu.SemaphoreType.DMA((2 * count + 9,)),
        ],
        4 * order * order * half,
        (place, *own, *other, *own_pieces, *other_pieces, moments, first, second),
    )


def direction_kernel(place_ref, *refs):
    own, other, (mine_hbm, theirs_hbm, out_hbm) = refs[:2], refs[2:4], refs[4:7]
    near, far, mine, theirs, out, semaphores = refs[7:]
    half = near.shape[0]
    upper, lower = pl.ds(0, half), pl.ds(half, half)
    first = place_ref[0] == 0
    copies = Copies(semaphores)
    waits = [
        copies.start(mine_hbm, mine),
        copies.start(theirs_hbm, theirs),
        copies.start_either(first, other[0].at[upper, :], own[1].at[lower, :], near),
        copies.start_either(first, other[1].at[upper, :], own[0].at[lower, :], far),
    ]
    for copy in waits:
        copy.wait()
    out[...] = (product(mine[...], near[...], NT) + product(theirs[...], far[...], NT)).astype(out.dtype)
    copies.start(out, out_hbm).wait()


def direction_step(place, own, other, mine, theirs):
    half = mine.shape[1]
    vmem = pltpu.VMEM
    square, rows = vmem((half, half), mine.dtype), vmem(mine.shape, mine.dtype)
    return kernel_call(
        direction_kernel,
        "direction_step",
        jax.ShapeDtypeStruct(mine.shape, mine.dtype),
        [square, square, rows, rows, rows, pltpu.SemaphoreType.DMA((5,))],
        4 * mine.shape[0] * half * half,
        (place, *own, *other, mine, theirs),
    )


def exchanged(block, axis, partner_of):
    count = lax.axis_size(axis)
    return lax.ppermute(block, axis, [(i, partner_of(i)) for i in range(count)])


def sibling(block):
    return exchanged(block, "dp", lambda i: i ^ 1)


def rounded_sum(x, y):
    return (x.astype(jnp.float32) + y.astype(jnp.float32)).astype(jnp.bfloat16)


def reversed_bits(value, bits):
    return sum(((value >> k) & 1) << (bits - 1 - k) for k in range(bits))


def pair_terms(partial_rows, half_width):
    side = lax.axis_index("dp") % 2
    blocks = lax.axis_size("dp") // 2
    bits = blocks.bit_length() - 1
    row_blocks, _, columns = partial_rows.shape
    halves = [
        partial_rows[rb, :, start : start + half_width]
        for rb in range(row_blocks)
        for start in range(0, columns, half_width)
    ]
    lows, highs = halves[0::2], halves[1::2]
    turned = [reversed_bits(k, bits) for k in range(blocks)]
    keep = jnp.stack([jnp.where(side == 0, lows[k], highs[turned[k]]) for k in range(blocks)])
    send = jnp.stack([jnp.where(side == 0, highs[turned[k]], lows[k]) for k in range(blocks)])
    return send, keep


def reduced_half_block(held, ahead):
    position = lax.axis_index("dp")
    side = position % 2
    bits = held.shape[0].bit_length() - 1
    for step in range(bits):
        low_bit, high_bit = 1 + step, bits - step
        mine = jnp.where(side == 0, position >> high_bit, position >> low_bit) & 1
        middle = held.shape[0] // 2
        keep = jnp.where(mine == 0, held[:middle], held[middle:])
        send = jnp.where(mine == 0, held[middle:], held[:middle])
        if step == bits - 1:
            send, ahead = lax.optimization_barrier((send, ahead))
        arrived = exchanged(send, "dp", lambda i: i ^ (1 << (low_bit if i % 2 else high_bit)))
        held = rounded_sum(keep, arrived)
    return held[0], ahead


def pieces_by_distance(shard, axis):
    count = lax.axis_size(axis)
    return [shard] + [
        lax.ppermute(shard, axis, [(i, (i + distance) % count) for i in range(count)]) for distance in range(1, count)
    ]


def body(grad_partial, factors, bases, first_moment, second_moment):
    row_count, block_width = factors.shape[1:]
    half_width = block_width // 2
    width = block_width // 4
    side = lax.axis_index("dp") % 2
    position, count = lax.axis_index("fsdp"), lax.axis_size("fsdp")
    place = jnp.stack([side, position]).astype(jnp.int32)
    bf16 = jnp.bfloat16

    send, keep = pair_terms(grad_partial[0], half_width)
    symmetric = row_count % 256 == 0 and count % 2 == 0
    share = gather_share(place, factors[0], bases[0], symmetric)
    pair_sum, share, first_rows = lax.optimization_barrier(
        (rounded_sum(keep, sibling(send)), share, bases[0, :, :width].astype(bf16))
    )
    gathered = lax.all_gather(share, "fsdp", axis=0, tiled=True)
    first_pieces = pieces_by_distance(first_rows, "fsdp")
    own_half, first_pieces = reduced_half_block(pair_sum, first_pieces)
    own_pieces = pieces_by_distance(own_half, "fsdp")
    other_pieces = [sibling(piece) for piece in own_pieces]

    moments = jnp.concatenate([first_moment[0].astype(bf16), second_moment[0].astype(bf16)], axis=1)
    rest, moments, own_pieces = lax.optimization_barrier((bases[0, :, half_width:].astype(bf16), moments, own_pieces))
    rest_pieces = pieces_by_distance(rest, "fsdp")
    moments = lax.all_gather(moments, "fsdp", axis=0, tiled=True)

    factor_whole, new_factor_rows, first_q = first_half(
        place, own_pieces, other_pieces, first_pieces, gathered, factors[0], count // 2 if symmetric else None
    )
    first_other = sibling(first_q)
    second_q, new_rows = second_half(place, rest_pieces, factor_whole, first_q)
    own, other = (first_q, second_q), (first_other, sibling(second_q))
    weighted, first_new, second_new = moment_step(
        place, own, other, own_pieces, other_pieces, moments, first_moment[0], second_moment[0]
    )
    direction = direction_step(place, own, other, weighted, sibling(weighted))
    return (new_factor_rows[None], new_rows[None], first_new[None], second_new[None], direction[None])


def solution(mesh):
    rows = P("dp", "fsdp", None)
    return jax.shard_map(
        body,
        mesh=mesh,
        in_specs=(P("dp", None, "fsdp", None), rows, rows, rows, rows),
        out_specs=(rows,) * 5,
        check_vma=False,
    )
```

time: 797 us -> 191 us (0.24)
  waiting for transfers between devices: 362 us -> 77.2 us
  other arithmetic: 267 us -> 7.53 us
  matrix products: 77.4 us -> 0 us
  Pallas kernels: 0 us -> 74.4 us
  local copies, waits for them, and re-layouts: 60.2 us -> 3.2 us
  starting transfers between devices: 2.81 us -> 14.3 us
    all_gather x6 -> x2, waiting for transfers between devices: 316 us -> 0.02 us  [the longest x1 0.02 us: body(): gathered = lax.all_gather(share, 'fsdp', axis=0, tiled=True)]
    another operation x33 -> x3, other arithmetic: 257 us -> 1.76 us  [the longest x1 1.1 us: pair_terms(): jnp.stack([jnp.where(side == 0, highs[turned[k]], lows[k]) for k in range...]
    pallas_call x0 -> x5, Pallas kernels: none -> 74.4 us  [the longest x4 72 us: kernel_call(): pl.pallas_call(kernel, out_shape=out_shape, in_specs=[SMEM] + [HBM] * (le...]
    ppermute x3 -> x19, waiting for transfers between devices: 2.91 us -> 77.1 us  [the longest x9 63.8 us: pieces_by_distance(): lax.ppermute(shard, axis, [(i, (i + distance) % count) for i in range(cou...]
    another operation x38 -> x0, local copies, waits for them, and re-layouts: 47.7 us -> none
    reduce_scatter x1 -> x0, waiting for transfers between devices: 42.4 us -> none  [body(): lax.psum_scatter(summand.astype(jnp.bfloat16), 'dp', scatter_dimension=0,...]
    another operation x29 -> x0, matrix products: 42.2 us -> none  [the longest x14 23.2 us: body(): cholesky_factor = jnp.linalg.cholesky(gram_matrix)]
    dot_general x6 -> x0, matrix products: 35.2 us -> none  [the longest x1 17.6 us: body(): lax.dot_general(power_whole, power_whole, (((0,), (0,)), ((), ())), preci...]
  transfers between devices with their start and end apart: 10 -> 21, of which waited for: 9 -> 11; matrix products, arithmetic and copies ran while one was open for 1% -> 1% of each run, Pallas kernels for 0% -> 33%
where the time goes in v1:
time: 191 us
  waiting for transfers between devices  77.2 us (40%)
  Pallas kernels  74.4 us (39%)
  between operations  14.4 us (8%)
  starting transfers between devices  14.3 us (7%)
  other arithmetic  7.53 us (4%)
  local copies, waits for them, and re-layouts  3.2 us (2%)
    pallas_call x4, Pallas kernels, kernel_call(): pl.pallas_call(kernel, out_shape=out_shape, in_specs=[SMEM] + [HBM] * (le...  72 us
    ppermute x9, waiting for transfers between devices, pieces_by_distance(): lax.ppermute(shard, axis, [(i, (i + distance) % count) for i in range(cou...  63.8 us
    ppermute x10, waiting for transfers between devices, exchanged(): return lax.ppermute(block, axis, [(i, partner_of(i)) for i in range(count)])  13.3 us
    ppermute x9, starting transfers between devices, pieces_by_distance(): lax.ppermute(shard, axis, [(i, (i + distance) % count) for i in range(cou...  7.81 us
    ppermute x10, starting transfers between devices, exchanged(): return lax.ppermute(block, axis, [(i, partner_of(i)) for i in range(count)])  6.44 us
  transfers between devices with their start and end apart: 21, of which 11 were waited for; matrix products, arithmetic and copies ran while one was open for 1% of the time, Pallas kernels for 33%

profile of v1, /device:TPU:13, one launch (start us, length us, event | category | flops | bytes accessed | tf_op | source)
XLA Modules:
  0.0 191.0 jit_solution(12838125261726021993)
XLA Ops:
  7.2 2.4 %broadcast_select_fusion.9 = (bf16[1,256,512]{2,1,0:T(8,128)(2,1)S(1)}, bf16[1,256,512]{2,1,0:T(8,128)(2,1)S(1)}, bf16[1,256,512]{2,1,0:T(8,128)(2,1)S(1)}, bf16...) fusion(pred[]{:T(512)S(6)} %eq.10, ...), kind=kLoop, calls=%fused_computation.16 | loop fusion | flops 1048576 | bytes 4194305 | tf_op jit(solution)/shard_map/jit(_where)/select_n | solution.py:528
  12.1 2.4 %gather_share.1 = bf16[256,896]{1,0:T(8,128)(2,1)} custom-call(s32[2]{0:T(128)} %pad_add_fusion.place_ref, f32[256,1024]{1,0:T(8,128)} %bitcast.24, f32[256,1024]{1,0:T(8,128)} %bitcast.20), custom_call_target="tpu_custom_call" | custom-call | bytes 3145728 | tf_op jit(solution)/shard_map/gather_share/pallas_call | solution.py:237
  14.5 1.3 add_convert_fusion
  16.7 1.2 collective-permute-start.1
  17.9 1.4 collective-permute-start.2
  20.3 1.5 collective-permute-start.4
  21.8 3.5 %collective-permute-done.1 = bf16[2,256,512]{2,1,0:T(8,128)(2,1)S(1)} collective-permute-done((bf16[2,256,512]{2,1,0:T(8,128)(2,1)}, bf16[2,256,512]{2,1,0:T(8,128)(2,1)S(1)}, u32[]{:S(2)}, u32[]{:S(2)}) %collective-permute-start.1) | collective-permute-done | bytes 524320 | tf_op jit(solution)/shard_map/ppermute | solution.py:501
  25.5 12.7 %collective-permute-done.3.refs_10_ = bf16[256,256]{1,0:T(8,128)(2,1)S(1)} collective-permute-done((bf16[256,256]{1,0:T(8,128)(2,1)S(1)}, bf16[256,256]{1,0:T(8,128)(2,1)S(1)}, u32[]{:S(2)}, u32[]{:S(2)}) %collective-permute-start.3) | collective-permute-done | bytes 131104 | tf_op jit(solution)/shard_map/ppermute | solution.py:553
  38.2 6.8 %collective-permute-done.4.refs_11_ = bf16[256,256]{1,0:T(8,128)(2,1)S(1)} collective-permute-done((bf16[256,256]{1,0:T(8,128)(2,1)S(1)}, bf16[256,256]{1,0:T(8,128)(2,1)S(1)}, u32[]{:S(2)}, u32[]{:S(2)}) %collective-permute-start.4) | collective-permute-done | bytes 131104 | tf_op jit(solution)/shard_map/ppermute | solution.py:553
  45.3 5.4 %collective-permute-done.5 = bf16[1,256,512]{2,1,0:T(8,128)(2,1)S(1)} collective-permute-done((bf16[1,256,512]{2,1,0:T(8,128)(2,1)S(1)}, bf16[1,256,512]{2,1,0:T(8,128)(2,1)S(1)}, u32[]{:S(2)}, u32[]{:S(2)}) %collective-permute-start.5) | collective-permute-done | bytes 262176 | tf_op jit(solution)/shard_map/ppermute | solution.py:501
  50.9 1.4 collective-permute-start.8
  53.2 23.3 %collective-permute-done.6.refs_1_.refs_5_ = bf16[256,512]{1,0:T(8,128)(2,1)S(1)} collective-permute-done((bf16[256,512]{1,0:T(8,128)(2,1)S(1)}, bf16[256,512]{1,0:T(8,128)(2,1)S(1)}, u32[]{:S(2)}, u32[]{:S(2)}) %collective-permute-start.6) | collective-permute-done | bytes 262176 | tf_op jit(solution)/shard_map/ppermute | solution.py:553
  76.5 6.4 %collective-permute-done.7.refs_2_.refs_6_ = bf16[256,512]{1,0:T(8,128)(2,1)S(1)} collective-permute-done((bf16[256,512]{1,0:T(8,128)(2,1)S(1)}, bf16[256,512]{1,0:T(8,128)(2,1)S(1)}, u32[]{:S(2)}, u32[]{:S(2)}) %collective-permute-start.7) | collective-permute-done | bytes 262176 | tf_op jit(solution)/shard_map/ppermute | solution.py:553
  82.9 1.7 collective-permute-done.8.refs_3_.refs_7_
  86.5 1.6 collective-permute-start.14
  89.8 31.5 %first_half.1 = (bf16[1024,1024]{1,0:T(8,128)(2,1)}, f32[256,1024]{1,0:T(8,128)}, bf16[1024,512]{1,0:T(8,128)(2,1)}) custom-call(s32[2]{0:T(128)} %pad_add_fusion.place_ref, bf16[1024,896]{1,0:T(8,128)(2,1)} %all-gather.3.cloned.1.call-done.gathered_hbm, f32[256,1024]{1,0:T(8,128)} %bitcast.25, bf16[256,512]{1,0:T(8,128)(2,1)} %copy-done.5, ...), custom_call_target="tpu_custom_call" | custom-call | flops 6442450944 | bytes 16777216 | tf_op jit(solution)/shard_map/first_half/pallas_call | solution.py:147
  121.3 1.3 collective-permute-start.16
  122.6 12.8 %collective-permute-done.15.refs_3_ = bf16[256,512]{1,0:T(8,128)(2,1)S(1)} collective-permute-done((bf16[256,512]{1,0:T(8,128)(2,1)S(1)}, bf16[256,512]{1,0:T(8,128)(2,1)S(1)}, u32[]{:S(2)}, u32[]{:S(2)}) %collective-permute-start.15) | collective-permute-done | bytes 262176 | tf_op jit(solution)/shard_map/ppermute | solution.py:553
  136.1 29.0 %second_half.1 = (bf16[1024,512]{1,0:T(8,128)(2,1)}, bf16[256,1024]{1,0:T(8,128)(2,1)}) custom-call(s32[2]{0:T(128)} %pad_add_fusion.place_ref, bf16[1024,1024]{1,0:T(8,128)(2,1)} %get-tuple-element.40.whole_hbm, bf16[1024,512]{1,0:T(8,128)(2,1)} %get-tuple-element.41.before_hbm.refs_0_, bf16[256,512]{1,0:T(8,128)(2,1)} %copy-done.14, ...), custom_call_target="tpu_custom_call" | custom-call | flops 4294967296 | bytes 16777216 | tf_op jit(solution)/shard_map/second_half/pallas_call | solution.py:147
  165.1 1.5 collective-permute-start.17
  166.7 2.5 %collective-permute-done.17.refs_3_ = bf16[1024,512]{1,0:T(8,128)(2,1)S(1)} collective-permute-done((bf16[1024,512]{1,0:T(8,128)(2,1)}, bf16[1024,512]{1,0:T(8,128)(2,1)S(1)}, u32[]{:S(2)}, u32[]{:S(2)}) %collective-permute-start.17) | collective-permute-done | bytes 1048608 | tf_op jit(solution)/shard_map/ppermute | solution.py:501
  170.1 8.3 %moment_step.1 = (bf16[256,512]{1,0:T(8,128)(2,1)}, f32[256,512]{1,0:T(8,128)}, f32[256,512]{1,0:T(8,128)}) custom-call(s32[2]{0:T(128)} %pad_add_fusion.place_ref, bf16[1024,512]{1,0:T(8,128)(2,1)} %get-tuple-element.41.before_hbm.refs_0_, bf16[1024,512]{1,0:T(8,128)(2,1)} %get-tuple-element.44.refs_1_, bf16[1024,512]{1,0:T(8,128)(2,1)} %copy-done, ...), custom_call_target="tpu_custom_call" | custom-call | flops 2147483648 | bytes 16777216 | tf_op jit(solution)/shard_map/moment_step/pallas_call | solution.py:147
  178.9 1.4 collective-permute-done.18.refs_5_
  180.9 3.2 %direction_step.1 = bf16[256,512]{1,0:T(8,128)(2,1)} custom-call(s32[2]{0:T(128)} %pad_add_fusion.place_ref, bf16[1024,512]{1,0:T(8,128)(2,1)} %get-tuple-element.41.before_hbm.refs_0_, bf16[1024,512]{1,0:T(8,128)(2,1)} %get-tuple-element.44.refs_1_, bf16[1024,512]{1,0:T(8,128)(2,1)} %copy-done, bf16[1024,512]{1,0:T(8,128)(2,1)} %copy-done.1, ...), custom_call_target="tpu_custom_call" | custom-call | flops 268435456 | bytes 16777216 | tf_op jit(solution)/shard_map/direction_step/pallas_call | solution.py:147
  (82 shorter events, 12.2 us)
Async XLA Ops:
  7.2 81.8 %all-gather.3.cloned.1.call-start = ((), (), s32[]{:S(2)}) async-start(), calls=%async_computation | async-start | bytes 2293760 | tf_op jit(solution)/shard_map/all_gather | solution.py:572
  10.7 3.8 %collective-permute-start = (bf16[4,256,512]{2,1,0:T(8,128)(2,1)}, bf16[4,256,512]{2,1,0:T(8,128)(2,1)S(1)}, u32[]{:S(2)}, u32[]{:S(2)}) collective-permute-start(bf16[4,256,512]{2,1,0:T(8,128)(2,1)} %pad_maximum_fusion), channel_id=1, source_target_pairs={{0,4},{4,0},{8,12},{12,8},{16,20},{20,16},{24,28},{28,24},{1,5},{5... | collective-permute-start | bytes 3145736 | tf_op jit(solution)/shard_map/ppermute | solution.py:501
  15.8 153.4 %all-gather.5.cloned.1.call-start = ((), (), s32[]{:S(2)}) async-start(), calls=%async_computation.1 | async-start | bytes 2621440 | tf_op jit(solution)/shard_map/all_gather | solution.py:581
  15.9 29.3 %copy-start.3 = (f32[1,256,512]{2,1,0:T(8,128)S(1)}, f32[1,256,512]{2,1,0:T(8,128)}, u32[]{:S(2)}) copy-start(f32[1,256,512]{2,1,0:T(8,128)} %param.9) | copy-start | bytes 1572868
  16.7 8.5 %collective-permute-start.1 = (bf16[2,256,512]{2,1,0:T(8,128)(2,1)}, bf16[2,256,512]{2,1,0:T(8,128)(2,1)S(1)}, u32[]{:S(2)}, u32[]{:S(2)}) collective-permute-start(bf16[2,256,512]{2,1,0:T(8,128)(2,1)} %broadcast_select_fusion), channel_id=1, source_target_pairs={{0,16},{4,12},{8,24},{12,4},{16,0},{20,28},{24,8},{28,20},{1,17},{... | collective-permute-start | bytes 1572872 | tf_op jit(solution)/shard_map/ppermute | solution.py:501
  17.9 7.6 %collective-permute-start.2 = (bf16[256,256]{1,0:T(8,128)(2,1)S(1)}, bf16[256,256]{1,0:T(8,128)(2,1)S(1)}, u32[]{:S(2)}, u32[]{:S(2)}) collective-permute-start(bf16[256,256]{1,0:T(8,128)(2,1)S(1)} %slice_bitcast_fusion.1.refs_8_), channel_id=1, source_target_pairs={{0,1},{1,2},{2,3},{3,0},{4,5},{5,6},{6,7},{7,4},{8,9},{9,10},{10,1... | collective-permute-start | bytes 393224 | tf_op jit(solution)/shard_map/ppermute | solution.py:553
  19.3 18.9 %collective-permute-start.3 = (bf16[256,256]{1,0:T(8,128)(2,1)S(1)}, bf16[256,256]{1,0:T(8,128)(2,1)S(1)}, u32[]{:S(2)}, u32[]{:S(2)}) collective-permute-start(bf16[256,256]{1,0:T(8,128)(2,1)S(1)} %slice_bitcast_fusion.1.refs_8_), channel_id=1, source_target_pairs={{0,2},{1,3},{2,0},{3,1},{4,6},{5,7},{6,4},{7,5},{8,10},{9,11},{10,... | collective-permute-start | bytes 393224 | tf_op jit(solution)/shard_map/ppermute | solution.py:553
  20.3 24.8 %collective-permute-start.4 = (bf16[256,256]{1,0:T(8,128)(2,1)S(1)}, bf16[256,256]{1,0:T(8,128)(2,1)S(1)}, u32[]{:S(2)}, u32[]{:S(2)}) collective-permute-start(bf16[256,256]{1,0:T(8,128)(2,1)S(1)} %slice_bitcast_fusion.1.refs_8_), channel_id=1, source_target_pairs={{0,3},{1,0},{2,1},{3,2},{4,7},{5,4},{6,5},{7,6},{8,11},{9,8},{10,9... | collective-permute-start | bytes 393224 | tf_op jit(solution)/shard_map/ppermute | solution.py:553
  45.1 5.6 %collective-permute-start.5 = (bf16[1,256,512]{2,1,0:T(8,128)(2,1)S(1)}, bf16[1,256,512]{2,1,0:T(8,128)(2,1)S(1)}, u32[]{:S(2)}, u32[]{:S(2)}) collective-permute-start(bf16[1,256,512]{2,1,0:T(8,128)(2,1)S(1)} %broadcast_select_fusion.1), channel_id=1, source_target_pairs={{0,8},{4,20},{8,0},{12,28},{16,24},{20,4},{24,16},{28,12},{1,9},{5... | collective-permute-start | bytes 786440 | tf_op jit(solution)/shard_map/ppermute | solution.py:501
  50.8 38.2 %copy-start.5 = (bf16[256,512]{1,0:T(8,128)(2,1)}, bf16[256,512]{1,0:T(8,128)(2,1)S(1)}, u32[]{:S(2)}) copy-start(bf16[256,512]{1,0:T(8,128)(2,1)S(1)} %fusion.refs_0_.refs_4_) | copy-start | bytes 786436
  50.8 25.7 %collective-permute-start.6 = (bf16[256,512]{1,0:T(8,128)(2,1)S(1)}, bf16[256,512]{1,0:T(8,128)(2,1)S(1)}, u32[]{:S(2)}, u32[]{:S(2)}) collective-permute-start(bf16[256,512]{1,0:T(8,128)(2,1)S(1)} %fusion.refs_0_.refs_4_), channel_id=1, source_target_pairs={{0,1},{1,2},{2,3},{3,0},{4,5},{5,6},{6,7},{7,4},{8,9},{9,10},{10,1... | collective-permute-start | bytes 786440 | tf_op jit(solution)/shard_map/ppermute | solution.py:553
  50.9 32.1 %collective-permute-start.7 = (bf16[256,512]{1,0:T(8,128)(2,1)S(1)}, bf16[256,512]{1,0:T(8,128)(2,1)S(1)}, u32[]{:S(2)}, u32[]{:S(2)}) collective-permute-start(bf16[256,512]{1,0:T(8,128)(2,1)S(1)} %fusion.refs_0_.refs_4_), channel_id=1, source_target_pairs={{0,2},{1,3},{2,0},{3,1},{4,6},{5,7},{6,4},{7,5},{8,10},{9,11},{10,... | collective-permute-start | bytes 786440 | tf_op jit(solution)/shard_map/ppermute | solution.py:553
  50.9 33.7 %collective-permute-start.8 = (bf16[256,512]{1,0:T(8,128)(2,1)S(1)}, bf16[256,512]{1,0:T(8,128)(2,1)S(1)}, u32[]{:S(2)}, u32[]{:S(2)}) collective-permute-start(bf16[256,512]{1,0:T(8,128)(2,1)S(1)} %fusion.refs_0_.refs_4_), channel_id=1, source_target_pairs={{0,3},{1,0},{2,1},{3,2},{4,7},{5,4},{6,5},{7,6},{8,11},{9,8},{10,9... | collective-permute-start | bytes 786440 | tf_op jit(solution)/shard_map/ppermute | solution.py:553
  53.2 68.1 %copy-start.14 = (bf16[256,512]{1,0:T(8,128)(2,1)}, bf16[256,512]{1,0:T(8,128)(2,1)S(1)}, u32[]{:S(2)}) copy-start(bf16[256,512]{1,0:T(8,128)(2,1)S(1)} %slice_bitcast_fusion.refs_0_) | copy-start | bytes 786436
  84.7 1.8 collective-permute-start.9
  85.3 2.7 %collective-permute-start.10 = (bf16[256,512]{1,0:T(8,128)(2,1)S(1)}, bf16[256,512]{1,0:T(8,128)(2,1)S(1)}, u32[]{:S(2)}, u32[]{:S(2)}) collective-permute-start(bf16[256,512]{1,0:T(8,128)(2,1)S(1)} %collective-permute-done.6.refs_1_.refs_5_), channel_id=1, source_target_pairs={{0,4},{4,0},{8,12},{12,8},{16,20},{20,16},{24,28},{28,24},{1,5},{5... | collective-permute-start | bytes 786440 | tf_op jit(solution)/shard_map/ppermute | solution.py:501
  85.4 3.6 %collective-permute-start.11 = (bf16[256,512]{1,0:T(8,128)(2,1)S(1)}, bf16[256,512]{1,0:T(8,128)(2,1)S(1)}, u32[]{:S(2)}, u32[]{:S(2)}) collective-permute-start(bf16[256,512]{1,0:T(8,128)(2,1)S(1)} %collective-permute-done.7.refs_2_.refs_6_), channel_id=1, source_target_pairs={{0,4},{4,0},{8,12},{12,8},{16,20},{20,16},{24,28},{28,24},{1,5},{5... | collective-permute-start | bytes 786440 | tf_op jit(solution)/shard_map/ppermute | solution.py:501
  85.8 3.1 %collective-permute-start.12 = (bf16[256,512]{1,0:T(8,128)(2,1)S(1)}, bf16[256,512]{1,0:T(8,128)(2,1)S(1)}, u32[]{:S(2)}, u32[]{:S(2)}) collective-permute-start(bf16[256,512]{1,0:T(8,128)(2,1)S(1)} %collective-permute-done.8.refs_3_.refs_7_), channel_id=1, source_target_pairs={{0,4},{4,0},{8,12},{12,8},{16,20},{20,16},{24,28},{28,24},{1,5},{5... | collective-permute-start | bytes 786440 | tf_op jit(solution)/shard_map/ppermute | solution.py:501
  85.9 36.7 %collective-permute-start.13 = (bf16[256,512]{1,0:T(8,128)(2,1)S(1)}, bf16[256,512]{1,0:T(8,128)(2,1)S(1)}, u32[]{:S(2)}, u32[]{:S(2)}) collective-permute-start(bf16[256,512]{1,0:T(8,128)(2,1)S(1)} %slice_bitcast_fusion.refs_0_), channel_id=1, source_target_pairs={{0,1},{1,2},{2,3},{3,0},{4,5},{5,6},{6,7},{7,4},{8,9},{9,10},{10,1... | collective-permute-start | bytes 786440 | tf_op jit(solution)/shard_map/ppermute | solution.py:553
  86.5 36.1 %collective-permute-start.14 = (bf16[256,512]{1,0:T(8,128)(2,1)S(1)}, bf16[256,512]{1,0:T(8,128)(2,1)S(1)}, u32[]{:S(2)}, u32[]{:S(2)}) collective-permute-start(bf16[256,512]{1,0:T(8,128)(2,1)S(1)} %slice_bitcast_fusion.refs_0_), channel_id=1, source_target_pairs={{0,2},{1,3},{2,0},{3,1},{4,6},{5,7},{6,4},{7,5},{8,10},{9,11},{10,... | collective-permute-start | bytes 786440 | tf_op jit(solution)/shard_map/ppermute | solution.py:553
  88.0 47.4 %collective-permute-start.15 = (bf16[256,512]{1,0:T(8,128)(2,1)S(1)}, bf16[256,512]{1,0:T(8,128)(2,1)S(1)}, u32[]{:S(2)}, u32[]{:S(2)}) collective-permute-start(bf16[256,512]{1,0:T(8,128)(2,1)S(1)} %slice_bitcast_fusion.refs_0_), channel_id=1, source_target_pairs={{0,3},{1,0},{2,1},{3,2},{4,7},{5,4},{6,5},{7,6},{8,11},{9,8},{10,9... | collective-permute-start | bytes 786440 | tf_op jit(solution)/shard_map/ppermute | solution.py:553
  121.3 45.4 %collective-permute-start.16 = (bf16[1024,512]{1,0:T(8,128)(2,1)}, bf16[1024,512]{1,0:T(8,128)(2,1)S(1)}, u32[]{:S(2)}, u32[]{:S(2)}) collective-permute-start(bf16[1024,512]{1,0:T(8,128)(2,1)} %get-tuple-element.41.before_hbm.refs_0_), channel_id=1, source_target_pairs={{0,4},{4,0},{8,12},{12,8},{16,20},{20,16},{24,28},{28,24},{1,5},{5... | collective-permute-start | bytes 3145736 | tf_op jit(solution)/shard_map/ppermute | solution.py:501
  165.1 4.0 %collective-permute-start.17 = (bf16[1024,512]{1,0:T(8,128)(2,1)}, bf16[1024,512]{1,0:T(8,128)(2,1)S(1)}, u32[]{:S(2)}, u32[]{:S(2)}) collective-permute-start(bf16[1024,512]{1,0:T(8,128)(2,1)} %get-tuple-element.44.refs_1_), channel_id=1, source_target_pairs={{0,4},{4,0},{8,12},{12,8},{16,20},{20,16},{24,28},{28,24},{1,5},{5... | collective-permute-start | bytes 3145736 | tf_op jit(solution)/shard_map/ppermute | solution.py:501
  178.4 1.8 collective-permute-start.18
  (19 other events, 127.7 us)
Sparse Core Ops, SparseCore 0:
  15.9 62.2 all-gather.2
  84.8 57.9 all-gather.4

commit v2 on v1

--- a/solution.py
+++ b/solution.py
@@ -36,22 +36,18 @@
     for p in range(0, SUB, 2):
         first, second = held[p], held[p + 1]
         a, b, c = splat_row(first, p), splat_row(second, p), splat_row(second, p + 1)
-        det = reciprocal(a * c - b * b)
-        ia, ib, ic = c * det, -b * det, a * det
+        inverse = reciprocal(a * c - b * b)
         at_first, at_second = sub == p, sub == p + 1
+        left = jnp.where(at_first, -c, jnp.where(at_second, b, c * first - b * second))
+        right = jnp.where(at_first, b, jnp.where(at_second, -a, a * second - b * first))
         for k in range(SUB):
             if k == p:
-                s, t = ia, ib
-                kept = jnp.zeros_like(first)
+                held[k] = -left * inverse
             elif k == p + 1:
-                s, t = ib, ic
-                kept = jnp.zeros_like(first)
+                held[k] = -right * inverse
             else:
-                u, v = splat_row(held[k], p), splat_row(held[k], p + 1)
-                s, t = ia * u + ib * v, ib * u + ic * v
-                kept = held[k]
-            rest = kept - (first * s + second * t)
-            held[k] = jnp.where(at_first, s, jnp.where(at_second, t, rest))
+                taken = left * splat_row(held[k], p) + right * splat_row(held[k], p + 1)
+                held[k] = jnp.where(at_first | at_second, 0.0, held[k]) - taken * inverse
     return held
 
 
@@ -195,20 +191,22 @@
         if start > 0:
             along = product(q_ref[:, :start], group.astype(bf16), TN).astype(bf16)
             group = group - product(q_ref[:, :start], along, NN)
-        group = group.astype(bf16)
+        group = (group * lax.rsqrt(jnp.sum(group * group, axis=0, keepdims=True))).astype(bf16)
         gram_ref[...] = product(group, group, TN)
         invert_factor(gram_ref)
         inverse = split_cat(gram_ref[...], "hl", 1)
         q_ref[:, span] = product(jnp.concatenate([group, group], axis=1), inverse, NT).astype(bf16)
 
 
-def share_kernel(symmetric, place_ref, factor_ref, basis_ref, share_ref):
+def share_kernel(symmetric, place_ref, factor_ref, basis_ref, early_ref, share_ref, late_ref):
     row_count, order = factor_ref.shape
     count = order // row_count
     width = order // 4
     bf16 = jnp.bfloat16
     shared = share_ref.shape[1] - width
+    early_ref[...] = basis_ref[:, :width].astype(bf16)
     share_ref[:, shared:] = basis_ref[:, width : 2 * width].astype(bf16)
+    late_ref[...] = basis_ref[:, 2 * width :].astype(bf16)
     if not symmetric:
         share_ref[:, :shared] = factor_ref[...].astype(bf16)
         return
@@ -230,18 +228,21 @@
             share_ref[:, count // 2 * row_count : shared] = last.astype(bf16)
 
 
-def gather_share(place, factor_rows, basis_rows, symmetric):
+def gather_shares(place, factor_rows, basis_rows, symmetric):
     row_count, order = factor_rows.shape
     shared = order // 2 + row_count // 2 if symmetric else order
     vmem = pl.BlockSpec(memory_space=pltpu.VMEM)
     return pl.pallas_call(
         functools.partial(share_kernel, symmetric),
-        out_shape=jax.ShapeDtypeStruct((row_count, shared + order // 4), jnp.bfloat16),
+        out_shape=tuple(
+            jax.ShapeDtypeStruct((row_count, columns), jnp.bfloat16)
+            for columns in (order // 4, shared + order // 4, order // 2)
+        ),
         in_specs=[SMEM, vmem, vmem],
-        out_specs=vmem,
+        out_specs=(vmem,) * 3,
         cost_estimate=pl.CostEstimate(flops=0, bytes_accessed=3 * 2**20, transcendentals=0),
         compiler_params=pltpu.CompilerParams(vmem_limit_bytes=VMEM_GRANT),
-        name="gather_share",
+        name="gather_shares",
     )(place, factor_rows, basis_rows)
 
 
@@ -530,7 +531,7 @@
     return send, keep
 
 
-def reduced_half_block(held, ahead):
+def reduced_half_block(held):
     position = lax.axis_index("dp")
     side = position % 2
     bits = held.shape[0].bit_length() - 1
@@ -540,11 +541,9 @@
         middle = held.shape[0] // 2
         keep = jnp.where(mine == 0, held[:middle], held[middle:])
         send = jnp.where(mine == 0, held[middle:], held[:middle])
-        if step == bits - 1:
-            send, ahead = lax.optimization_barrier((send, ahead))
         arrived = exchanged(send, "dp", lambda i: i ^ (1 << (low_bit if i % 2 else high_bit)))
         held = rounded_sum(keep, arrived)
-    return held[0], ahead
+    return held[0]
 
 
 def pieces_by_distance(shard, axis):
@@ -557,34 +556,31 @@
 def body(grad_partial, factors, bases, first_moment, second_moment):
     row_count, block_width = factors.shape[1:]
     half_width = block_width // 2
-    width = block_width // 4
     side = lax.axis_index("dp") % 2
     position, count = lax.axis_index("fsdp"), lax.axis_size("fsdp")
     place = jnp.stack([side, position]).astype(jnp.int32)
     bf16 = jnp.bfloat16
 
+    symmetric = row_count % 256 == 0 and count % 2 == 0
+    early, share, late = gather_shares(place, factors[0], bases[0], symmetric)
+    first_pieces = pieces_by_distance(early, "fsdp")
+    gathered = lax.all_gather(share, "fsdp", axis=0, tiled=True)
     send, keep = pair_terms(grad_partial[0], half_width)
-    symmetric = row_count % 256 == 0 and count % 2 == 0
-    share = gather_share(place, factors[0], bases[0], symmetric)
-    pair_sum, share, first_rows = lax.optimization_barrier(
-        (rounded_sum(keep, sibling(send)), share, bases[0, :, :width].astype(bf16))
-    )
-    gathered = lax.all_gather(share, "fsdp", axis=0, tiled=True)
-    first_pieces = pieces_by_distance(first_rows, "fsdp")
-    own_half, first_pieces = reduced_half_block(pair_sum, first_pieces)
+    pair_sum, first_pieces[1] = lax.optimization_barrier((rounded_sum(keep, sibling(send)), first_pieces[1]))
+    own_half, first_pieces = lax.optimization_barrier((reduced_half_block(pair_sum), first_pieces))
     own_pieces = pieces_by_distance(own_half, "fsdp")
     other_pieces = [sibling(piece) for piece in own_pieces]
 
     moments = jnp.concatenate([first_moment[0].astype(bf16), second_moment[0].astype(bf16)], axis=1)
-    rest, moments, own_pieces = lax.optimization_barrier((bases[0, :, half_width:].astype(bf16), moments, own_pieces))
-    rest_pieces = pieces_by_distance(rest, "fsdp")
+    late, moments, own_pieces = lax.optimization_barrier((late, moments, own_pieces))
+    late_pieces = pieces_by_distance(late, "fsdp")
     moments = lax.all_gather(moments, "fsdp", axis=0, tiled=True)
 
     factor_whole, new_factor_rows, first_q = first_half(
         place, own_pieces, other_pieces, first_pieces, gathered, factors[0], count // 2 if symmetric else None
     )
     first_other = sibling(first_q)
-    second_q, new_rows = second_half(place, rest_pieces, factor_whole, first_q)
+    second_q, new_rows = second_half(place, late_pieces, factor_whole, first_q)
     own, other = (first_q, second_q), (first_other, sibling(second_q))
     weighted, first_new, second_new = moment_step(
         place, own, other, own_pieces, other_pieces, moments, first_moment[0], second_moment[0]

time: 191 us -> 188 us (0.984)
  waiting for transfers between devices: 77.2 us -> 81.1 us
  other arithmetic: 7.53 us -> 4.01 us
  Pallas kernels: 74.4 us -> 71.2 us
    pallas_call x4, Pallas kernels: 72 us -> 68.7 us  [kernel_call(): pl.pallas_call(kernel, out_shape=out_shape, in_specs=[SMEM] + [HBM] * (le...]
    ppermute x9, waiting for transfers between devices: 63.8 us -> 66.6 us  [pieces_by_distance(): lax.ppermute(shard, axis, [(i, (i + distance) % count) for i in range(cou...]
  transfers between devices with their start and end apart: 21 -> 21, of which waited for: 11 -> 12; matrix products, arithmetic and copies ran while one was open for 1% -> 1% of each run, Pallas kernels for 33% -> 32%
where the time goes in v2:
time: 188 us
  waiting for transfers between devices  81.1 us (43%)
  Pallas kernels  71.2 us (38%)
  between operations  14.3 us (8%)
  starting transfers between devices  13.8 us (7%)
  other arithmetic  4.01 us (2%)
  local copies, waits for them, and re-layouts  3.11 us (2%)
    pallas_call x4, Pallas kernels, kernel_call(): pl.pallas_call(kernel, out_shape=out_shape, in_specs=[SMEM] + [HBM] * (le...  68.7 us
    ppermute x9, waiting for transfers between devices, pieces_by_distance(): lax.ppermute(shard, axis, [(i, (i + distance) % count) for i in range(cou...  66.6 us
    ppermute x10, waiting for transfers between devices, exchanged(): return lax.ppermute(block, axis, [(i, partner_of(i)) for i in range(count)])  14.4 us
    ppermute x9, starting transfers between devices, pieces_by_distance(): lax.ppermute(shard, axis, [(i, (i + distance) % count) for i in range(cou...  7.2 us
    ppermute x10, starting transfers between devices, exchanged(): return lax.ppermute(block, axis, [(i, partner_of(i)) for i in range(count)])  6.56 us
  transfers between devices with their start and end apart: 21, of which 12 were waited for; matrix products, arithmetic and copies ran while one was open for 1% of the time, Pallas kernels for 32%

profile of v2, /device:TPU:13, one launch (start us, length us, event | category | flops | bytes accessed | tf_op | source)
XLA Modules:
  0.0 187.6 jit_solution(10219759204620790394)
XLA Ops:
  7.2 1.7 broadcast_select_fusion.8
  10.4 2.6 %gather_shares.1 = (bf16[256,256]{1,0:T(8,128)(2,1)}, bf16[256,896]{1,0:T(8,128)(2,1)}, bf16[256,512]{1,0:T(8,128)(2,1)}) custom-call(s32[2]{0:T(128)} %pad_add_fusion.place_ref, f32[256,1024]{1,0:T(8,128)} %bitcast.20, f32[256,1024]{1,0:T(8,128)} %bitcast.19), custom_call_target="tpu_custom_call" | custom-call | bytes 3145728 | tf_op jit(solution)/shard_map/gather_shares/pallas_call | solution.py:235
  13.0 1.4 collective-permute-start.1
  14.7 3.7 %collective-permute-done.1.refs_9_ = bf16[256,256]{1,0:T(8,128)(2,1)S(1)} collective-permute-done((bf16[256,256]{1,0:T(8,128)(2,1)}, bf16[256,256]{1,0:T(8,128)(2,1)S(1)}, u32[]{:S(2)}, u32[]{:S(2)}) %collective-permute-start.1) | collective-permute-done | bytes 131104 | tf_op jit(solution)/shard_map/ppermute | solution.py:552
  18.5 1.3 collective-permute-start.2
  19.8 7.2 %collective-permute-done.2 = bf16[2,256,512]{2,1,0:T(8,128)(2,1)S(1)} collective-permute-done((bf16[2,256,512]{2,1,0:T(8,128)(2,1)S(1)}, bf16[2,256,512]{2,1,0:T(8,128)(2,1)S(1)}, u32[]{:S(2)}, u32[]{:S(2)}) %collective-permute-start.2) | collective-permute-done | bytes 524320 | tf_op jit(solution)/shard_map/ppermute | solution.py:502
  27.5 2.4 %collective-permute-start.4 = (bf16[256,256]{1,0:T(8,128)(2,1)S(1)}, bf16[256,256]{1,0:T(8,128)(2,1)S(1)}, u32[]{:S(2)}, u32[]{:S(2)}) collective-permute-start(bf16[256,256]{1,0:T(8,128)(2,1)S(1)} %copy-done.17), channel_id=1, source_target_pairs={{0,2},{1,3},{2,0},{3,1},{4,6},{5,7},{6,4},{7,5},{8,10},{9,11},{10,... | collective-permute-start | bytes 393224 | tf_op jit(solution)/shard_map/ppermute | solution.py:552
  30.1 2.8 %collective-permute-done.3 = bf16[1,256,512]{2,1,0:T(8,128)(2,1)S(1)} collective-permute-done((bf16[1,256,512]{2,1,0:T(8,128)(2,1)S(1)}, bf16[1,256,512]{2,1,0:T(8,128)(2,1)S(1)}, u32[]{:S(2)}, u32[]{:S(2)}) %collective-permute-start.3) | collective-permute-done | bytes 262176 | tf_op jit(solution)/shard_map/ppermute | solution.py:502
  32.9 12.4 %collective-permute-done.4.refs_10_ = bf16[256,256]{1,0:T(8,128)(2,1)S(1)} collective-permute-done((bf16[256,256]{1,0:T(8,128)(2,1)S(1)}, bf16[256,256]{1,0:T(8,128)(2,1)S(1)}, u32[]{:S(2)}, u32[]{:S(2)}) %collective-permute-start.4) | collective-permute-done | bytes 131104 | tf_op jit(solution)/shard_map/ppermute | solution.py:552
  45.3 8.6 %collective-permute-done.5.refs_11_ = bf16[256,256]{1,0:T(8,128)(2,1)S(1)} collective-permute-done((bf16[256,256]{1,0:T(8,128)(2,1)S(1)}, bf16[256,256]{1,0:T(8,128)(2,1)S(1)}, u32[]{:S(2)}, u32[]{:S(2)}) %collective-permute-start.5) | collective-permute-done | bytes 131104 | tf_op jit(solution)/shard_map/ppermute | solution.py:552
  53.9 1.5 collective-permute-start.8
  56.3 19.8 %collective-permute-done.6.refs_1_.refs_5_ = bf16[256,512]{1,0:T(8,128)(2,1)S(1)} collective-permute-done((bf16[256,512]{1,0:T(8,128)(2,1)S(1)}, bf16[256,512]{1,0:T(8,128)(2,1)S(1)}, u32[]{:S(2)}, u32[]{:S(2)}) %collective-permute-start.6) | collective-permute-done | bytes 262176 | tf_op jit(solution)/shard_map/ppermute | solution.py:552
  76.2 5.6 %collective-permute-done.7.refs_2_.refs_6_ = bf16[256,512]{1,0:T(8,128)(2,1)S(1)} collective-permute-done((bf16[256,512]{1,0:T(8,128)(2,1)S(1)}, bf16[256,512]{1,0:T(8,128)(2,1)S(1)}, u32[]{:S(2)}, u32[]{:S(2)}) %collective-permute-start.7) | collective-permute-done | bytes 262176 | tf_op jit(solution)/shard_map/ppermute | solution.py:552
  81.8 2.9 %collective-permute-done.8.refs_3_.refs_7_ = bf16[256,512]{1,0:T(8,128)(2,1)S(1)} collective-permute-done((bf16[256,512]{1,0:T(8,128)(2,1)S(1)}, bf16[256,512]{1,0:T(8,128)(2,1)S(1)}, u32[]{:S(2)}, u32[]{:S(2)}) %collective-permute-start.8) | collective-permute-done | bytes 262176 | tf_op jit(solution)/shard_map/ppermute | solution.py:552
  87.6 0.9 collective-permute-start.15
  89.3 29.9 %first_half.1 = (bf16[1024,1024]{1,0:T(8,128)(2,1)}, f32[256,1024]{1,0:T(8,128)}, bf16[1024,512]{1,0:T(8,128)(2,1)}) custom-call(s32[2]{0:T(128)} %pad_add_fusion.place_ref, bf16[1024,896]{1,0:T(8,128)(2,1)} %all-gather.3.cloned.1.call-done.gathered_hbm, f32[256,1024]{1,0:T(8,128)} %bitcast.21, bf16[256,512]{1,0:T(8,128)(2,1)} %copy-done.4, ...), custom_call_target="tpu_custom_call" | custom-call | flops 6442450944 | bytes 16777216 | tf_op jit(solution)/shard_map/first_half/pallas_call | solution.py:143
  119.2 1.5 collective-permute-start.16
  120.7 13.7 %collective-permute-done.15.refs_3_ = bf16[256,512]{1,0:T(8,128)(2,1)S(1)} collective-permute-done((bf16[256,512]{1,0:T(8,128)(2,1)S(1)}, bf16[256,512]{1,0:T(8,128)(2,1)S(1)}, u32[]{:S(2)}, u32[]{:S(2)}) %collective-permute-start.15) | collective-permute-done | bytes 262176 | tf_op jit(solution)/shard_map/ppermute | solution.py:552
  135.1 27.3 %second_half.1 = (bf16[1024,512]{1,0:T(8,128)(2,1)}, bf16[256,1024]{1,0:T(8,128)(2,1)}) custom-call(s32[2]{0:T(128)} %pad_add_fusion.place_ref, bf16[1024,1024]{1,0:T(8,128)(2,1)} %get-tuple-element.44.whole_hbm, bf16[1024,512]{1,0:T(8,128)(2,1)} %get-tuple-element.45.before_hbm.refs_0_, bf16[256,512]{1,0:T(8,128)(2,1)} %get-tuple-element.46.refs_0_, ...), custom_call_target="tpu_custom_call" | custom-call | flops 4294967296 | bytes 16777216 | tf_op jit(solution)/shard_map/second_half/pallas_call | solution.py:143
  163.3 2.5 %collective-permute-done.17.refs_3_ = bf16[1024,512]{1,0:T(8,128)(2,1)S(1)} collective-permute-done((bf16[1024,512]{1,0:T(8,128)(2,1)}, bf16[1024,512]{1,0:T(8,128)(2,1)S(1)}, u32[]{:S(2)}, u32[]{:S(2)}) %collective-permute-start.17) | collective-permute-done | bytes 1048608 | tf_op jit(solution)/shard_map/ppermute | solution.py:502
  165.8 1.0 copy-done.1
  166.7 8.3 %moment_step.1 = (bf16[256,512]{1,0:T(8,128)(2,1)}, f32[256,512]{1,0:T(8,128)}, f32[256,512]{1,0:T(8,128)}) custom-call(s32[2]{0:T(128)} %pad_add_fusion.place_ref, bf16[1024,512]{1,0:T(8,128)(2,1)} %get-tuple-element.45.before_hbm.refs_0_, bf16[1024,512]{1,0:T(8,128)(2,1)} %get-tuple-element.48.refs_1_, bf16[1024,512]{1,0:T(8,128)(2,1)} %copy-done, ...), custom_call_target="tpu_custom_call" | custom-call | flops 2147483648 | bytes 16777216 | tf_op jit(solution)/shard_map/moment_step/pallas_call | solution.py:143
  175.5 1.4 collective-permute-done.18.refs_5_
  177.6 3.2 %direction_step.1 = bf16[256,512]{1,0:T(8,128)(2,1)} custom-call(s32[2]{0:T(128)} %pad_add_fusion.place_ref, bf16[1024,512]{1,0:T(8,128)(2,1)} %get-tuple-element.45.before_hbm.refs_0_, bf16[1024,512]{1,0:T(8,128)(2,1)} %get-tuple-element.48.refs_1_, bf16[1024,512]{1,0:T(8,128)(2,1)} %copy-done, bf16[1024,512]{1,0:T(8,128)(2,1)} %copy-done.1, ...), custom_call_target="tpu_custom_call" | custom-call | flops 268435456 | bytes 16777216 | tf_op jit(solution)/shard_map/direction_step/pallas_call | solution.py:143
  (77 shorter events, 10.0 us)
Async XLA Ops:
  7.2 81.4 %all-gather.3.cloned.1.call-start = ((), (), s32[]{:S(2)}) async-start(), calls=%async_computation | async-start | bytes 2293760 | tf_op jit(solution)/shard_map/all_gather | solution.py:567
  9.1 5.4 %collective-permute-start = (bf16[4,256,512]{2,1,0:T(8,128)(2,1)S(1)}, bf16[4,256,512]{2,1,0:T(8,128)(2,1)S(1)}, u32[]{:S(2)}, u32[]{:S(2)}) collective-permute-start(bf16[4,256,512]{2,1,0:T(8,128)(2,1)S(1)} %pad_maximum_fusion), channel_id=1, source_target_pairs={{0,4},{4,0},{8,12},{12,8},{16,20},{20,16},{24,28},{28,24},{1,5},{5... | collective-permute-start | bytes 3145736 | tf_op jit(solution)/shard_map/ppermute | solution.py:502
  13.0 152.8 %all-gather.5.cloned.1.call-start = ((), (), s32[]{:S(2)}) async-start(), calls=%async_computation.1 | async-start | bytes 2621440 | tf_op jit(solution)/shard_map/all_gather | solution.py:577
  13.0 5.4 %collective-permute-start.1 = (bf16[256,256]{1,0:T(8,128)(2,1)}, bf16[256,256]{1,0:T(8,128)(2,1)S(1)}, u32[]{:S(2)}, u32[]{:S(2)}) collective-permute-start(bf16[256,256]{1,0:T(8,128)(2,1)} %get-tuple-element.39.refs_8_), channel_id=1, source_target_pairs={{0,1},{1,2},{2,3},{3,0},{4,5},{5,6},{6,7},{7,4},{8,9},{9,10},{10,1... | collective-permute-start | bytes 393224 | tf_op jit(solution)/shard_map/ppermute | solution.py:552
  18.5 8.5 %collective-permute-start.2 = (bf16[2,256,512]{2,1,0:T(8,128)(2,1)S(1)}, bf16[2,256,512]{2,1,0:T(8,128)(2,1)S(1)}, u32[]{:S(2)}, u32[]{:S(2)}) collective-permute-start(bf16[2,256,512]{2,1,0:T(8,128)(2,1)S(1)} %broadcast_select_fusion), channel_id=1, source_target_pairs={{0,16},{4,12},{8,24},{12,4},{16,0},{20,28},{24,8},{28,20},{1,17},{... | collective-permute-start | bytes 1572872 | tf_op jit(solution)/shard_map/ppermute | solution.py:502
  27.2 58.9 %copy-start.13 = (bf16[256,512]{1,0:T(8,128)(2,1)S(1)}, bf16[256,512]{1,0:T(8,128)(2,1)}, u32[]{:S(2)}) copy-start(bf16[256,512]{1,0:T(8,128)(2,1)} %get-tuple-element.46.refs_0_) | copy-start | bytes 786436
  27.2 5.6 %collective-permute-start.3 = (bf16[1,256,512]{2,1,0:T(8,128)(2,1)S(1)}, bf16[1,256,512]{2,1,0:T(8,128)(2,1)S(1)}, u32[]{:S(2)}, u32[]{:S(2)}) collective-permute-start(bf16[1,256,512]{2,1,0:T(8,128)(2,1)S(1)} %broadcast_select_fusion.9), channel_id=1, source_target_pairs={{0,8},{4,20},{8,0},{12,28},{16,24},{20,4},{24,16},{28,12},{1,9},{5... | collective-permute-start | bytes 786440 | tf_op jit(solution)/shard_map/ppermute | solution.py:502
  27.5 17.8 %collective-permute-start.4 = (bf16[256,256]{1,0:T(8,128)(2,1)S(1)}, bf16[256,256]{1,0:T(8,128)(2,1)S(1)}, u32[]{:S(2)}, u32[]{:S(2)}) collective-permute-start(bf16[256,256]{1,0:T(8,128)(2,1)S(1)} %copy-done.17), channel_id=1, source_target_pairs={{0,2},{1,3},{2,0},{3,1},{4,6},{5,7},{6,4},{7,5},{8,10},{9,11},{10,... | collective-permute-start | bytes 393224 | tf_op jit(solution)/shard_map/ppermute | solution.py:552
  29.9 24.0 %collective-permute-start.5 = (bf16[256,256]{1,0:T(8,128)(2,1)S(1)}, bf16[256,256]{1,0:T(8,128)(2,1)S(1)}, u32[]{:S(2)}, u32[]{:S(2)}) collective-permute-start(bf16[256,256]{1,0:T(8,128)(2,1)S(1)} %copy-done.17), channel_id=1, source_target_pairs={{0,3},{1,0},{2,1},{3,2},{4,7},{5,4},{6,5},{7,6},{8,11},{9,8},{10,9... | collective-permute-start | bytes 393224 | tf_op jit(solution)/shard_map/ppermute | solution.py:552
  32.9 55.6 %copy-start.4 = (bf16[256,512]{1,0:T(8,128)(2,1)}, bf16[256,512]{1,0:T(8,128)(2,1)S(1)}, u32[]{:S(2)}) copy-start(bf16[256,512]{1,0:T(8,128)(2,1)S(1)} %fusion.refs_0_.refs_4_) | copy-start | bytes 786436
  45.3 43.3 %copy-start.19 = (bf16[256,256]{1,0:T(8,128)(2,1)}, bf16[256,256]{1,0:T(8,128)(2,1)S(1)}, u32[]{:S(2)}) copy-start(bf16[256,256]{1,0:T(8,128)(2,1)S(1)} %collective-permute-done.4.refs_10_) | copy-start | bytes 393220
  53.9 22.2 %collective-permute-start.6 = (bf16[256,512]{1,0:T(8,128)(2,1)S(1)}, bf16[256,512]{1,0:T(8,128)(2,1)S(1)}, u32[]{:S(2)}, u32[]{:S(2)}) collective-permute-start(bf16[256,512]{1,0:T(8,128)(2,1)S(1)} %fusion.refs_0_.refs_4_), channel_id=1, source_target_pairs={{0,1},{1,2},{2,3},{3,0},{4,5},{5,6},{6,7},{7,4},{8,9},{9,10},{10,1... | collective-permute-start | bytes 786440 | tf_op jit(solution)/shard_map/ppermute | solution.py:552
  53.9 27.9 %collective-permute-start.7 = (bf16[256,512]{1,0:T(8,128)(2,1)S(1)}, bf16[256,512]{1,0:T(8,128)(2,1)S(1)}, u32[]{:S(2)}, u32[]{:S(2)}) collective-permute-start(bf16[256,512]{1,0:T(8,128)(2,1)S(1)} %fusion.refs_0_.refs_4_), channel_id=1, source_target_pairs={{0,2},{1,3},{2,0},{3,1},{4,6},{5,7},{6,4},{7,5},{8,10},{9,11},{10,... | collective-permute-start | bytes 786440 | tf_op jit(solution)/shard_map/ppermute | solution.py:552
  53.9 30.7 %collective-permute-start.8 = (bf16[256,512]{1,0:T(8,128)(2,1)S(1)}, bf16[256,512]{1,0:T(8,128)(2,1)S(1)}, u32[]{:S(2)}, u32[]{:S(2)}) collective-permute-start(bf16[256,512]{1,0:T(8,128)(2,1)S(1)} %fusion.refs_0_.refs_4_), channel_id=1, source_target_pairs={{0,3},{1,0},{2,1},{3,2},{4,7},{5,4},{6,5},{7,6},{8,11},{9,8},{10,9... | collective-permute-start | bytes 786440 | tf_op jit(solution)/shard_map/ppermute | solution.py:552
  84.7 2.0 %collective-permute-start.9 = (bf16[256,512]{1,0:T(8,128)(2,1)S(1)}, bf16[256,512]{1,0:T(8,128)(2,1)S(1)}, u32[]{:S(2)}, u32[]{:S(2)}) collective-permute-start(bf16[256,512]{1,0:T(8,128)(2,1)S(1)} %fusion.refs_0_.refs_4_), channel_id=1, source_target_pairs={{0,4},{4,0},{8,12},{12,8},{16,20},{20,16},{24,28},{28,24},{1,5},{5... | collective-permute-start | bytes 786440 | tf_op jit(solution)/shard_map/ppermute | solution.py:502
  85.5 2.1 %collective-permute-start.10 = (bf16[256,512]{1,0:T(8,128)(2,1)S(1)}, bf16[256,512]{1,0:T(8,128)(2,1)S(1)}, u32[]{:S(2)}, u32[]{:S(2)}) collective-permute-start(bf16[256,512]{1,0:T(8,128)(2,1)S(1)} %collective-permute-done.6.refs_1_.refs_5_), channel_id=1, source_target_pairs={{0,4},{4,0},{8,12},{12,8},{16,20},{20,16},{24,28},{28,24},{1,5},{5... | collective-permute-start | bytes 786440 | tf_op jit(solution)/shard_map/ppermute | solution.py:502
  85.6 2.9 %collective-permute-start.11 = (bf16[256,512]{1,0:T(8,128)(2,1)S(1)}, bf16[256,512]{1,0:T(8,128)(2,1)S(1)}, u32[]{:S(2)}, u32[]{:S(2)}) collective-permute-start(bf16[256,512]{1,0:T(8,128)(2,1)S(1)} %collective-permute-done.7.refs_2_.refs_6_), channel_id=1, source_target_pairs={{0,4},{4,0},{8,12},{12,8},{16,20},{20,16},{24,28},{28,24},{1,5},{5... | collective-permute-start | bytes 786440 | tf_op jit(solution)/shard_map/ppermute | solution.py:502
  86.1 2.5 %collective-permute-start.12 = (bf16[256,512]{1,0:T(8,128)(2,1)S(1)}, bf16[256,512]{1,0:T(8,128)(2,1)S(1)}, u32[]{:S(2)}, u32[]{:S(2)}) collective-permute-start(bf16[256,512]{1,0:T(8,128)(2,1)S(1)} %collective-permute-done.8.refs_3_.refs_7_), channel_id=1, source_target_pairs={{0,4},{4,0},{8,12},{12,8},{16,20},{20,16},{24,28},{28,24},{1,5},{5... | collective-permute-start | bytes 786440 | tf_op jit(solution)/shard_map/ppermute | solution.py:502
  86.1 34.5 %collective-permute-start.13 = (bf16[256,512]{1,0:T(8,128)(2,1)S(1)}, bf16[256,512]{1,0:T(8,128)(2,1)S(1)}, u32[]{:S(2)}, u32[]{:S(2)}) collective-permute-start(bf16[256,512]{1,0:T(8,128)(2,1)S(1)} %copy-done.13), channel_id=1, source_target_pairs={{0,1},{1,2},{2,3},{3,0},{4,5},{5,6},{6,7},{7,4},{8,9},{9,10},{10,1... | collective-permute-start | bytes 786440 | tf_op jit(solution)/shard_map/ppermute | solution.py:552
  86.7 34.0 %collective-permute-start.14 = (bf16[256,512]{1,0:T(8,128)(2,1)S(1)}, bf16[256,512]{1,0:T(8,128)(2,1)S(1)}, u32[]{:S(2)}, u32[]{:S(2)}) collective-permute-start(bf16[256,512]{1,0:T(8,128)(2,1)S(1)} %copy-done.13), channel_id=1, source_target_pairs={{0,2},{1,3},{2,0},{3,1},{4,6},{5,7},{6,4},{7,5},{8,10},{9,11},{10,... | collective-permute-start | bytes 786440 | tf_op jit(solution)/shard_map/ppermute | solution.py:552
  87.6 46.8 %collective-permute-start.15 = (bf16[256,512]{1,0:T(8,128)(2,1)S(1)}, bf16[256,512]{1,0:T(8,128)(2,1)S(1)}, u32[]{:S(2)}, u32[]{:S(2)}) collective-permute-start(bf16[256,512]{1,0:T(8,128)(2,1)S(1)} %copy-done.13), channel_id=1, source_target_pairs={{0,3},{1,0},{2,1},{3,2},{4,7},{5,4},{6,5},{7,6},{8,11},{9,8},{10,9... | collective-permute-start | bytes 786440 | tf_op jit(solution)/shard_map/ppermute | solution.py:552
  119.2 44.1 %collective-permute-start.16 = (bf16[1024,512]{1,0:T(8,128)(2,1)}, bf16[1024,512]{1,0:T(8,128)(2,1)S(1)}, u32[]{:S(2)}, u32[]{:S(2)}) collective-permute-start(bf16[1024,512]{1,0:T(8,128)(2,1)} %get-tuple-element.45.before_hbm.refs_0_), channel_id=1, source_target_pairs={{0,4},{4,0},{8,12},{12,8},{16,20},{20,16},{24,28},{28,24},{1,5},{5... | collective-permute-start | bytes 3145736 | tf_op jit(solution)/shard_map/ppermute | solution.py:502
  162.4 3.4 %collective-permute-start.17 = (bf16[1024,512]{1,0:T(8,128)(2,1)}, bf16[1024,512]{1,0:T(8,128)(2,1)S(1)}, u32[]{:S(2)}, u32[]{:S(2)}) collective-permute-start(bf16[1024,512]{1,0:T(8,128)(2,1)} %get-tuple-element.48.refs_1_), channel_id=1, source_target_pairs={{0,4},{4,0},{8,12},{12,8},{16,20},{20,16},{24,28},{28,24},{1,5},{5... | collective-permute-start | bytes 3145736 | tf_op jit(solution)/shard_map/ppermute | solution.py:502
  175.0 1.8 collective-permute-start.18
  (18 other events, 190.1 us)
Sparse Core Ops, SparseCore 0:
  13.1 61.7 all-gather.2
  84.8 58.2 all-gather.4

commit v3 on v2

--- a/solution.py
+++ b/solution.py
@@ -336,17 +336,13 @@
     )
 
 
-def second_kernel(count, place_ref, whole_hbm, before_hbm, *refs):
-    basis, (q_hbm, rows_hbm) = refs[:count], refs[count : count + 2]
-    whole, before, columns, power, q, gram, semaphores = refs[count + 2 :]
+def second_kernel(row_count, place_ref, columns_hbm, whole_hbm, before_hbm, q_hbm, rows_hbm, *refs):
+    whole, before, columns, power, q, gram, semaphores = refs
     order, half = before.shape
-    row_count = order // count
     bf16 = jnp.bfloat16
-    here = rows_from(place_ref[1], 0, row_count, count)
+    here = rows_from(place_ref[1], 0, row_count, order // row_count)
     copies = Copies(semaphores)
-    waits = [copies.start(whole_hbm, whole)]
-    for k in range(count):
-        waits.append(copies.start(basis[k], columns.at[rows_from(place_ref[1], k, row_count, count), :]))
+    waits = [copies.start(whole_hbm, whole), copies.start(columns_hbm, columns)]
     last = copies.start(before_hbm, before)
     for copy in waits:
         copy.wait()
@@ -362,13 +358,12 @@
         copy.wait()
 
 
-def second_half(place, basis, whole, before):
+def second_half(place, columns, whole, before, row_count):
     order, half = before.shape
-    row_count = order // len(basis)
     bf16, f32 = jnp.bfloat16, jnp.float32
     shape, vmem = jax.ShapeDtypeStruct, pltpu.VMEM
     return kernel_call(
-        functools.partial(second_kernel, len(basis)),
+        functools.partial(second_kernel, row_count),
         "second_half",
         (shape((order, half), bf16), shape((row_count, order), bf16)),
         [
@@ -378,10 +373,10 @@
             vmem((order, half), f32),
             vmem((order, half), bf16),
             vmem((half // 2, half // 2), f32),
-            pltpu.SemaphoreType.DMA((len(basis) + 5,)),
+            pltpu.SemaphoreType.DMA((6,)),
         ],
         4 * order**3,
-        (place, whole, before, *basis),
+        (place, columns, whole, before),
     )
 
 
@@ -531,7 +526,7 @@
     return send, keep
 
 
-def reduced_half_block(held):
+def reduced_half_block(held, ahead):
     position = lax.axis_index("dp")
     side = position % 2
     bits = held.shape[0].bit_length() - 1
@@ -541,9 +536,11 @@
         middle = held.shape[0] // 2
         keep = jnp.where(mine == 0, held[:middle], held[middle:])
         send = jnp.where(mine == 0, held[middle:], held[:middle])
+        if step == 0:
+            send, ahead = lax.optimization_barrier((send, ahead))
         arrived = exchanged(send, "dp", lambda i: i ^ (1 << (low_bit if i % 2 else high_bit)))
         held = rounded_sum(keep, arrived)
-    return held[0]
+    return held[0], ahead
 
 
 def pieces_by_distance(shard, axis):
@@ -565,22 +562,21 @@
     early, share, late = gather_shares(place, factors[0], bases[0], symmetric)
     first_pieces = pieces_by_distance(early, "fsdp")
     gathered = lax.all_gather(share, "fsdp", axis=0, tiled=True)
+    late = lax.all_gather(late, "fsdp", axis=0, tiled=True)
     send, keep = pair_terms(grad_partial[0], half_width)
-    pair_sum, first_pieces[1] = lax.optimization_barrier((rounded_sum(keep, sibling(send)), first_pieces[1]))
-    own_half, first_pieces = lax.optimization_barrier((reduced_half_block(pair_sum), first_pieces))
+    pair_sum = rounded_sum(keep, sibling(send))
+    own_half, first_pieces = reduced_half_block(pair_sum, first_pieces)
+    moments = jnp.concatenate([first_moment[0].astype(bf16), second_moment[0].astype(bf16)], axis=1)
+    moments, own_half = lax.optimization_barrier((moments, own_half))
+    moments = lax.all_gather(moments, "fsdp", axis=0, tiled=True)
     own_pieces = pieces_by_distance(own_half, "fsdp")
     other_pieces = [sibling(piece) for piece in own_pieces]
 
-    moments = jnp.concatenate([first_moment[0].astype(bf16), second_moment[0].astype(bf16)], axis=1)
-    late, moments, own_pieces = lax.optimization_barrier((late, moments, own_pieces))
-    late_pieces = pieces_by_distance(late, "fsdp")
-    moments = lax.all_gather(moments, "fsdp", axis=0, tiled=True)
-
     factor_whole, new_factor_rows, first_q = first_half(
         place, own_pieces, other_pieces, first_pieces, gathered, factors[0], count // 2 if symmetric else None
     )
     first_other = sibling(first_q)
-    second_q, new_rows = second_half(place, late_pieces, factor_whole, first_q)
+    second_q, new_rows = second_half(place, late, factor_whole, first_q, row_count)
     own, other = (first_q, second_q), (first_other, sibling(second_q))
     weighted, first_new, second_new = moment_step(
         place, own, other, own_pieces, other_pieces, moments, first_moment[0], second_moment[0]

time: 188 us -> 169 us (0.90); the launches traced: 188 us -> 166 us
  waiting for transfers between devices: 81.1 us -> 54.3 us
  starting transfers between devices: 13.8 us -> 22.8 us
    ppermute x9 -> x6, waiting for transfers between devices: 66.6 us -> 33.5 us  [pieces_by_distance(): lax.ppermute(shard, axis, [(i, (i + distance) % count) for i in range(cou...]
    ppermute x10, starting transfers between devices: 6.56 us -> 17.4 us  [exchanged(): return lax.ppermute(block, axis, [(i, partner_of(i)) for i in range(count)])]
    all_gather x1, waiting for transfers between devices: 0.01 us -> 3.91 us  [body(): moments = lax.all_gather(moments, 'fsdp', axis=0, tiled=True)]
    ppermute x10, waiting for transfers between devices: 14.4 us -> 16.8 us  [exchanged(): return lax.ppermute(block, axis, [(i, partner_of(i)) for i in range(count)])]
    ppermute x9 -> x6, starting transfers between devices: 7.2 us -> 5.34 us  [pieces_by_distance(): lax.ppermute(shard, axis, [(i, (i + distance) % count) for i in range(cou...]
  transfers between devices with their start and end apart: 21 -> 19, of which waited for: 12 -> 12; matrix products, arithmetic and copies ran while one was open for 1% -> 1% of each run, Pallas kernels for 32% -> 34%
where the time goes in v3:
time: 169 us; the launch traced here: 166 us
  Pallas kernels  71.1 us (42%)
  waiting for transfers between devices  54.3 us (32%)
  starting transfers between devices  22.8 us (13%)
  between operations  14 us (8%)
  other arithmetic  2.55 us (2%)
    pallas_call x4, Pallas kernels, kernel_call(): pl.pallas_call(kernel, out_shape=out_shape, in_specs=[SMEM] + [HBM] * (le...  68.6 us
    ppermute x6, waiting for transfers between devices, pieces_by_distance(): lax.ppermute(shard, axis, [(i, (i + distance) % count) for i in range(cou...  33.5 us
    ppermute x10, starting transfers between devices, exchanged(): return lax.ppermute(block, axis, [(i, partner_of(i)) for i in range(count)])  17.4 us
    ppermute x10, waiting for transfers between devices, exchanged(): return lax.ppermute(block, axis, [(i, partner_of(i)) for i in range(count)])  16.8 us
    ppermute x6, starting transfers between devices, pieces_by_distance(): lax.ppermute(shard, axis, [(i, (i + distance) % count) for i in range(cou...  5.34 us
    all_gather x1, waiting for transfers between devices, body(): moments = lax.all_gather(moments, 'fsdp', axis=0, tiled=True)  3.91 us
  transfers between devices with their start and end apart: 19, of which 12 were waited for; matrix products, arithmetic and copies ran while one was open for 1% of the time, Pallas kernels for 34%

profile of v3, /device:TPU:13, one launch (start us, length us, event | category | flops | bytes accessed | tf_op | source)
XLA Modules:
  0.0 166.2 jit_solution(7200047231532698261)
XLA Ops:
  7.9 2.6 %gather_shares.1 = (bf16[256,256]{1,0:T(8,128)(2,1)}, bf16[256,896]{1,0:T(8,128)(2,1)}, bf16[256,512]{1,0:T(8,128)(2,1)}) custom-call(s32[2]{0:T(128)} %pad_add_fusion.place_ref, f32[256,1024]{1,0:T(8,128)} %bitcast.20, f32[256,1024]{1,0:T(8,128)} %bitcast.19), custom_call_target="tpu_custom_call" | custom-call | bytes 3145728 | tf_op jit(solution)/shard_map/gather_shares/pallas_call | solution.py:235
  11.6 1.4 collective-permute-start.1
  13.0 1.0 collective-permute-start.2
  14.0 1.5 collective-permute-start.3
  16.0 12.4 %collective-permute-done.2.refs_10_ = bf16[256,256]{1,0:T(8,128)(2,1)S(1)} collective-permute-done((bf16[256,256]{1,0:T(8,128)(2,1)S(1)}, bf16[256,256]{1,0:T(8,128)(2,1)S(1)}, u32[]{:S(2)}, u32[]{:S(2)}) %collective-permute-start.2) | collective-permute-done | bytes 131104 | tf_op jit(solution)/shard_map/ppermute | solution.py:549
  28.3 7.8 %collective-permute-done.3.refs_11_ = bf16[256,256]{1,0:T(8,128)(2,1)} collective-permute-done((bf16[256,256]{1,0:T(8,128)(2,1)S(1)}, bf16[256,256]{1,0:T(8,128)(2,1)}, u32[]{:S(2)}, u32[]{:S(2)}) %collective-permute-start.3) | collective-permute-done | bytes 131104 | tf_op jit(solution)/shard_map/ppermute | solution.py:549
  36.2 1.2 collective-permute-start.4
  37.5 7.1 %collective-permute-done.4 = bf16[2,256,512]{2,1,0:T(8,128)(2,1)S(1)} collective-permute-done((bf16[2,256,512]{2,1,0:T(8,128)(2,1)S(1)}, bf16[2,256,512]{2,1,0:T(8,128)(2,1)S(1)}, u32[]{:S(2)}, u32[]{:S(2)}) %collective-permute-start.4) | collective-permute-done | bytes 524320 | tf_op jit(solution)/shard_map/ppermute | solution.py:497
  46.1 4.5 %collective-permute-done.5 = bf16[1,256,512]{2,1,0:T(8,128)(2,1)S(1)} collective-permute-done((bf16[1,256,512]{2,1,0:T(8,128)(2,1)S(1)}, bf16[1,256,512]{2,1,0:T(8,128)(2,1)S(1)}, u32[]{:S(2)}, u32[]{:S(2)}) %collective-permute-start.5) | collective-permute-done | bytes 262176 | tf_op jit(solution)/shard_map/ppermute | solution.py:497
  50.8 1.4 collective-permute-start.8
  52.2 8.7 %collective-permute-start.9 = (bf16[256,512]{1,0:T(8,128)(2,1)S(1)}, bf16[256,512]{1,0:T(8,128)(2,1)S(1)}, u32[]{:S(2)}, u32[]{:S(2)}) collective-permute-start(bf16[256,512]{1,0:T(8,128)(2,1)S(1)} %fusion.refs_0_.refs_4_), channel_id=1, source_target_pairs={{0,4},{4,0},{8,12},{12,8},{16,20},{20,16},{24,28},{28,24},{1,5},{5... | collective-permute-start | bytes 786440 | tf_op jit(solution)/shard_map/ppermute | solution.py:497
  60.9 9.2 %collective-permute-done.6.refs_1_.refs_5_ = bf16[256,512]{1,0:T(8,128)(2,1)S(1)} collective-permute-done((bf16[256,512]{1,0:T(8,128)(2,1)S(1)}, bf16[256,512]{1,0:T(8,128)(2,1)S(1)}, u32[]{:S(2)}, u32[]{:S(2)}) %collective-permute-start.6) | collective-permute-done | bytes 262176 | tf_op jit(solution)/shard_map/ppermute | solution.py:549
  70.1 2.6 %collective-permute-start.10 = (bf16[256,512]{1,0:T(8,128)(2,1)S(1)}, bf16[256,512]{1,0:T(8,128)(2,1)S(1)}, u32[]{:S(2)}, u32[]{:S(2)}) collective-permute-start(bf16[256,512]{1,0:T(8,128)(2,1)S(1)} %collective-permute-done.6.refs_1_.refs_5_), channel_id=1, source_target_pairs={{0,4},{4,0},{8,12},{12,8},{16,20},{20,16},{24,28},{28,24},{1,5},{5... | collective-permute-start | bytes 786440 | tf_op jit(solution)/shard_map/ppermute | solution.py:497
  72.7 3.1 %collective-permute-done.7.refs_2_.refs_6_ = bf16[256,512]{1,0:T(8,128)(2,1)S(1)} collective-permute-done((bf16[256,512]{1,0:T(8,128)(2,1)S(1)}, bf16[256,512]{1,0:T(8,128)(2,1)S(1)}, u32[]{:S(2)}, u32[]{:S(2)}) %collective-permute-start.7) | collective-permute-done | bytes 262176 | tf_op jit(solution)/shard_map/ppermute | solution.py:549
  75.8 1.5 collective-permute-start.11
  79.0 1.1 collective-permute-done.12.refs_7_.refs_11_
  80.8 29.7 %first_half.1 = (bf16[1024,1024]{1,0:T(8,128)(2,1)}, f32[256,1024]{1,0:T(8,128)}, bf16[1024,512]{1,0:T(8,128)(2,1)}) custom-call(s32[2]{0:T(128)} %pad_add_fusion.place_ref, bf16[1024,896]{1,0:T(8,128)(2,1)} %all-gather.4.cloned.1.call-done.gathered_hbm, f32[256,1024]{1,0:T(8,128)} %bitcast.21, bf16[256,512]{1,0:T(8,128)(2,1)} %copy-done.5, ...), custom_call_target="tpu_custom_call" | custom-call | flops 6442450944 | bytes 16777216 | tf_op jit(solution)/shard_map/first_half/pallas_call | solution.py:143
  111.0 27.3 %second_half.1 = (bf16[1024,512]{1,0:T(8,128)(2,1)}, bf16[256,1024]{1,0:T(8,128)(2,1)}) custom-call(s32[2]{0:T(128)} %pad_add_fusion.place_ref, bf16[1024,512]{1,0:T(8,128)(2,1)} %all-gather.6.cloned.1.call-done.columns_hbm, bf16[1024,1024]{1,0:T(8,128)(2,1)} %get-tuple-element.33.whole_hbm, bf16[1024,512]{1,0:T(8,128)(2,1)} %get-tuple-element.34.before_hbm.refs_0_), custom_call_target="tpu_custom_call" | custom-call | flops 4294967296 | bytes 16777216 | tf_op jit(solution)/shard_map/second_half/pallas_call | solution.py:143
  138.6 2.7 %collective-permute-done.14.refs_3_ = bf16[1024,512]{1,0:T(8,128)(2,1)S(1)} collective-permute-done((bf16[1024,512]{1,0:T(8,128)(2,1)}, bf16[1024,512]{1,0:T(8,128)(2,1)S(1)}, u32[]{:S(2)}, u32[]{:S(2)}) %collective-permute-start.14) | collective-permute-done | bytes 1048608 | tf_op jit(solution)/shard_map/ppermute | solution.py:497
  141.3 3.9 %all-gather.8.cloned.1.call-done.refs_12_ = bf16[1024,1024]{1,0:T(8,128)(2,1)} async-done(((bf16[256,1024]{1,0:T(8,128)(2,1)}), bf16[1024,1024]{1,0:T(8,128)(2,1)}) %all-gather.8.cloned.1.call-update) | async-done | bytes 2097168 | tf_op jit(solution)/shard_map/all_gather | solution.py:571
  145.2 8.3 %moment_step.1 = (bf16[256,512]{1,0:T(8,128)(2,1)}, f32[256,512]{1,0:T(8,128)}, f32[256,512]{1,0:T(8,128)}) custom-call(s32[2]{0:T(128)} %pad_add_fusion.place_ref, bf16[1024,512]{1,0:T(8,128)(2,1)} %get-tuple-element.34.before_hbm.refs_0_, bf16[1024,512]{1,0:T(8,128)(2,1)} %get-tuple-element.36.refs_1_, bf16[1024,512]{1,0:T(8,128)(2,1)} %copy-done, ...), custom_call_target="tpu_custom_call" | custom-call | flops 2147483648 | bytes 16777216 | tf_op jit(solution)/shard_map/moment_step/pallas_call | solution.py:143
  153.5 0.9 collective-permute-start.15
  154.4 1.4 collective-permute-done.15.refs_5_
  156.5 3.2 %direction_step.1 = bf16[256,512]{1,0:T(8,128)(2,1)} custom-call(s32[2]{0:T(128)} %pad_add_fusion.place_ref, bf16[1024,512]{1,0:T(8,128)(2,1)} %get-tuple-element.34.before_hbm.refs_0_, bf16[1024,512]{1,0:T(8,128)(2,1)} %get-tuple-element.36.refs_1_, bf16[1024,512]{1,0:T(8,128)(2,1)} %copy-done, bf16[1024,512]{1,0:T(8,128)(2,1)} %copy-done.1, ...), custom_call_target="tpu_custom_call" | custom-call | flops 268435456 | bytes 16777216 | tf_op jit(solution)/shard_map/direction_step/pallas_call | solution.py:143
  (66 shorter events, 7.7 us)
Async XLA Ops:
  7.2 72.9 %all-gather.4.cloned.1.call-start = ((), (), s32[]{:S(2)}) async-start(), calls=%async_computation | async-start | bytes 2293760 | tf_op jit(solution)/shard_map/all_gather | solution.py:564
  10.5 100.6 %all-gather.6.cloned.1.call-start = ((), (), s32[]{:S(2)}) async-start(), calls=%async_computation.1 | async-start | bytes 1310720 | tf_op jit(solution)/shard_map/all_gather | solution.py:565
  10.9 4.6 %collective-permute-start = (bf16[4,256,512]{2,1,0:T(8,128)(2,1)S(1)}, bf16[4,256,512]{2,1,0:T(8,128)(2,1)S(1)}, u32[]{:S(2)}, u32[]{:S(2)}) collective-permute-start(bf16[4,256,512]{2,1,0:T(8,128)(2,1)S(1)} %pad_maximum_fusion), channel_id=1, source_target_pairs={{0,4},{4,0},{8,12},{12,8},{16,20},{20,16},{24,28},{28,24},{1,5},{5... | collective-permute-start | bytes 3145736 | tf_op jit(solution)/shard_map/ppermute | solution.py:497
  11.6 4.4 %collective-permute-start.1 = (bf16[256,256]{1,0:T(8,128)(2,1)S(1)}, bf16[256,256]{1,0:T(8,128)(2,1)S(1)}, u32[]{:S(2)}, u32[]{:S(2)}) collective-permute-start(bf16[256,256]{1,0:T(8,128)(2,1)S(1)} %copy-done.14), channel_id=1, source_target_pairs={{0,1},{1,2},{2,3},{3,0},{4,5},{5,6},{6,7},{7,4},{8,9},{9,10},{10,1... | collective-permute-start | bytes 393224 | tf_op jit(solution)/shard_map/ppermute | solution.py:549
  13.0 15.4 %collective-permute-start.2 = (bf16[256,256]{1,0:T(8,128)(2,1)S(1)}, bf16[256,256]{1,0:T(8,128)(2,1)S(1)}, u32[]{:S(2)}, u32[]{:S(2)}) collective-permute-start(bf16[256,256]{1,0:T(8,128)(2,1)S(1)} %copy-done.14), channel_id=1, source_target_pairs={{0,2},{1,3},{2,0},{3,1},{4,6},{5,7},{6,4},{7,5},{8,10},{9,11},{10,... | collective-permute-start | bytes 393224 | tf_op jit(solution)/shard_map/ppermute | solution.py:549
  14.0 22.2 %collective-permute-start.3 = (bf16[256,256]{1,0:T(8,128)(2,1)S(1)}, bf16[256,256]{1,0:T(8,128)(2,1)}, u32[]{:S(2)}, u32[]{:S(2)}) collective-permute-start(bf16[256,256]{1,0:T(8,128)(2,1)S(1)} %copy-done.14), channel_id=1, source_target_pairs={{0,3},{1,0},{2,1},{3,2},{4,7},{5,4},{6,5},{7,6},{8,11},{9,8},{10,9... | collective-permute-start | bytes 393224 | tf_op jit(solution)/shard_map/ppermute | solution.py:549
  15.7 29.4 %copy-start.2 = (f32[1,256,512]{2,1,0:T(8,128)S(1)}, f32[1,256,512]{2,1,0:T(8,128)}, u32[]{:S(2)}) copy-start(f32[1,256,512]{2,1,0:T(8,128)} %param.9) | copy-start | bytes 1572868
  15.8 29.3 %copy-start.3 = (f32[1,256,512]{2,1,0:T(8,128)S(1)}, f32[1,256,512]{2,1,0:T(8,128)}, u32[]{:S(2)}) copy-start(f32[1,256,512]{2,1,0:T(8,128)} %param.8) | copy-start | bytes 1572868
  16.0 29.2 %copy-start.15 = (bf16[256,256]{1,0:T(8,128)(2,1)}, bf16[256,256]{1,0:T(8,128)(2,1)S(1)}, u32[]{:S(2)}) copy-start(bf16[256,256]{1,0:T(8,128)(2,1)S(1)} %collective-permute-done.1.refs_9_) | copy-start | bytes 393220
  28.3 16.8 %copy-start.16 = (bf16[256,256]{1,0:T(8,128)(2,1)}, bf16[256,256]{1,0:T(8,128)(2,1)S(1)}, u32[]{:S(2)}) copy-start(bf16[256,256]{1,0:T(8,128)(2,1)S(1)} %collective-permute-done.2.refs_10_) | copy-start | bytes 393220
  36.2 8.4 %collective-permute-start.4 = (bf16[2,256,512]{2,1,0:T(8,128)(2,1)S(1)}, bf16[2,256,512]{2,1,0:T(8,128)(2,1)S(1)}, u32[]{:S(2)}, u32[]{:S(2)}) collective-permute-start(bf16[2,256,512]{2,1,0:T(8,128)(2,1)S(1)} %broadcast_select_fusion), channel_id=1, source_target_pairs={{0,16},{4,12},{8,24},{12,4},{16,0},{20,28},{24,8},{28,20},{1,17},{... | collective-permute-start | bytes 1572872 | tf_op jit(solution)/shard_map/ppermute | solution.py:497
  37.4 107.8 %all-gather.8.cloned.1.call-start = ((), (), s32[]{:S(2)}) async-start(), calls=%async_computation.2 | async-start | bytes 2621440 | tf_op jit(solution)/shard_map/all_gather | solution.py:571
  44.9 5.7 %collective-permute-start.5 = (bf16[1,256,512]{2,1,0:T(8,128)(2,1)S(1)}, bf16[1,256,512]{2,1,0:T(8,128)(2,1)S(1)}, u32[]{:S(2)}, u32[]{:S(2)}) collective-permute-start(bf16[1,256,512]{2,1,0:T(8,128)(2,1)S(1)} %broadcast_select_fusion.9), channel_id=1, source_target_pairs={{0,8},{4,20},{8,0},{12,28},{16,24},{20,4},{24,16},{28,12},{1,9},{5... | collective-permute-start | bytes 786440 | tf_op jit(solution)/shard_map/ppermute | solution.py:497
  50.7 29.5 %copy-start.5 = (bf16[256,512]{1,0:T(8,128)(2,1)}, bf16[256,512]{1,0:T(8,128)(2,1)S(1)}, u32[]{:S(2)}) copy-start(bf16[256,512]{1,0:T(8,128)(2,1)S(1)} %fusion.refs_0_.refs_4_) | copy-start | bytes 786436
  50.7 19.4 %collective-permute-start.6 = (bf16[256,512]{1,0:T(8,128)(2,1)S(1)}, bf16[256,512]{1,0:T(8,128)(2,1)S(1)}, u32[]{:S(2)}, u32[]{:S(2)}) collective-permute-start(bf16[256,512]{1,0:T(8,128)(2,1)S(1)} %fusion.refs_0_.refs_4_), channel_id=1, source_target_pairs={{0,1},{1,2},{2,3},{3,0},{4,5},{5,6},{6,7},{7,4},{8,9},{9,10},{10,1... | collective-permute-start | bytes 786440 | tf_op jit(solution)/shard_map/ppermute | solution.py:549
  50.8 25.1 %collective-permute-start.7 = (bf16[256,512]{1,0:T(8,128)(2,1)S(1)}, bf16[256,512]{1,0:T(8,128)(2,1)S(1)}, u32[]{:S(2)}, u32[]{:S(2)}) collective-permute-start(bf16[256,512]{1,0:T(8,128)(2,1)S(1)} %fusion.refs_0_.refs_4_), channel_id=1, source_target_pairs={{0,2},{1,3},{2,0},{3,1},{4,6},{5,7},{6,4},{7,5},{8,10},{9,11},{10,... | collective-permute-start | bytes 786440 | tf_op jit(solution)/shard_map/ppermute | solution.py:549
  50.8 27.3 %collective-permute-start.8 = (bf16[256,512]{1,0:T(8,128)(2,1)S(1)}, bf16[256,512]{1,0:T(8,128)(2,1)S(1)}, u32[]{:S(2)}, u32[]{:S(2)}) collective-permute-start(bf16[256,512]{1,0:T(8,128)(2,1)S(1)} %fusion.refs_0_.refs_4_), channel_id=1, source_target_pairs={{0,3},{1,0},{2,1},{3,2},{4,7},{5,4},{6,5},{7,6},{8,11},{9,8},{10,9... | collective-permute-start | bytes 786440 | tf_op jit(solution)/shard_map/ppermute | solution.py:549
  52.2 26.7 %collective-permute-start.9 = (bf16[256,512]{1,0:T(8,128)(2,1)S(1)}, bf16[256,512]{1,0:T(8,128)(2,1)S(1)}, u32[]{:S(2)}, u32[]{:S(2)}) collective-permute-start(bf16[256,512]{1,0:T(8,128)(2,1)S(1)} %fusion.refs_0_.refs_4_), channel_id=1, source_target_pairs={{0,4},{4,0},{8,12},{12,8},{16,20},{20,16},{24,28},{28,24},{1,5},{5... | collective-permute-start | bytes 786440 | tf_op jit(solution)/shard_map/ppermute | solution.py:497
  70.1 8.9 %collective-permute-start.10 = (bf16[256,512]{1,0:T(8,128)(2,1)S(1)}, bf16[256,512]{1,0:T(8,128)(2,1)S(1)}, u32[]{:S(2)}, u32[]{:S(2)}) collective-permute-start(bf16[256,512]{1,0:T(8,128)(2,1)S(1)} %collective-permute-done.6.refs_1_.refs_5_), channel_id=1, source_target_pairs={{0,4},{4,0},{8,12},{12,8},{16,20},{20,16},{24,28},{28,24},{1,5},{5... | collective-permute-start | bytes 786440 | tf_op jit(solution)/shard_map/ppermute | solution.py:497
  75.8 3.2 %collective-permute-start.11 = (bf16[256,512]{1,0:T(8,128)(2,1)S(1)}, bf16[256,512]{1,0:T(8,128)(2,1)S(1)}, u32[]{:S(2)}, u32[]{:S(2)}) collective-permute-start(bf16[256,512]{1,0:T(8,128)(2,1)S(1)} %collective-permute-done.7.refs_2_.refs_6_), channel_id=1, source_target_pairs={{0,4},{4,0},{8,12},{12,8},{16,20},{20,16},{24,28},{28,24},{1,5},{5... | collective-permute-start | bytes 786440 | tf_op jit(solution)/shard_map/ppermute | solution.py:497
  78.1 2.0 %collective-permute-start.12 = (bf16[256,512]{1,0:T(8,128)(2,1)S(1)}, bf16[256,512]{1,0:T(8,128)(2,1)S(1)}, u32[]{:S(2)}, u32[]{:S(2)}) collective-permute-start(bf16[256,512]{1,0:T(8,128)(2,1)S(1)} %collective-permute-done.8.refs_3_.refs_7_), channel_id=1, source_target_pairs={{0,4},{4,0},{8,12},{12,8},{16,20},{20,16},{24,28},{28,24},{1,5},{5... | collective-permute-start | bytes 786440 | tf_op jit(solution)/shard_map/ppermute | solution.py:497
  110.6 28.0 %collective-permute-start.13 = (bf16[1024,512]{1,0:T(8,128)(2,1)}, bf16[1024,512]{1,0:T(8,128)(2,1)S(1)}, u32[]{:S(2)}, u32[]{:S(2)}) collective-permute-start(bf16[1024,512]{1,0:T(8,128)(2,1)} %get-tuple-element.34.before_hbm.refs_0_), channel_id=1, source_target_pairs={{0,4},{4,0},{8,12},{12,8},{16,20},{20,16},{24,28},{28,24},{1,5},{5... | collective-permute-start | bytes 3145736 | tf_op jit(solution)/shard_map/ppermute | solution.py:497
  138.4 2.9 %collective-permute-start.14 = (bf16[1024,512]{1,0:T(8,128)(2,1)}, bf16[1024,512]{1,0:T(8,128)(2,1)S(1)}, u32[]{:S(2)}, u32[]{:S(2)}) collective-permute-start(bf16[1024,512]{1,0:T(8,128)(2,1)} %get-tuple-element.36.refs_1_), channel_id=1, source_target_pairs={{0,4},{4,0},{8,12},{12,8},{16,20},{20,16},{24,28},{28,24},{1,5},{5... | collective-permute-start | bytes 3145736 | tf_op jit(solution)/shard_map/ppermute | solution.py:497
  153.5 2.3 %collective-permute-start.15 = (bf16[256,512]{1,0:T(8,128)(2,1)}, bf16[256,512]{1,0:T(8,128)(2,1)S(1)}, u32[]{:S(2)}, u32[]{:S(2)}) collective-permute-start(bf16[256,512]{1,0:T(8,128)(2,1)} %get-tuple-element.40.refs_4_), channel_id=1, source_target_pairs={{0,4},{4,0},{8,12},{12,8},{16,20},{20,16},{24,28},{28,24},{1,5},{5... | collective-permute-start | bytes 786440 | tf_op jit(solution)/shard_map/ppermute | solution.py:497
  (12 other events, 36.2 us)
Sparse Core Ops, SparseCore 0:
  10.6 45.3 all-gather.3
  58.1 40.4 all-gather.5
  100.8 44.3 all-gather.7

commit v4 on v3

--- a/solution.py
+++ b/solution.py
@@ -380,49 +380,106 @@
     )
 
 
-def moment_kernel(count, place_ref, *refs):
-    own, other, own_pieces, other_pieces = refs[:2], refs[2:4], refs[4 : 4 + count], refs[4 + count : 4 + 2 * count]
-    moments_hbm, first_hbm, second_hbm = refs[4 + 2 * count : 7 + 2 * count]
-    weighted_hbm, first_out, second_out = refs[7 + 2 * count : 10 + 2 * count]
-    left, right, block, moments, first_rows, second_rows, mixed, rotated, normal, weighted, semaphores = refs[
-        10 + 2 * count :
-    ]
+def rotate_kernel(count, place_ref, own_first, own_second, other_first, *refs):
+    own_pieces, other_pieces, (mixed_hbm, upper_hbm) = refs[:count], refs[count : 2 * count], refs[2 * count : 2 * count + 2]
+    left, right, block, mixed, rotated, semaphores = refs[2 * count + 2 :]
+    order, half_width = left.shape
+    first = place_ref[0] == 0
+    upper, lower = pl.ds(0, half_width), pl.ds(half_width, half_width)
+    copies = Copies(semaphores)
+    waits = [copies.start_either(first, other_first, own_second, right)]
+    for k in range(count):
+        span = rows_from(place_ref[1], k, order // count, count)
+        waits.append(copies.start_either(first, own_pieces[k], other_pieces[k], block.at[span, upper]))
+        waits.append(copies.start_either(first, other_pieces[k], own_pieces[k], block.at[span, lower]))
+    last = copies.start_either(first, own_first, other_first, left)
+    for copy in waits:
+        copy.wait()
+    mixed[...] = product(block[...], right[...], NN).astype(mixed.dtype)
+    outputs = [copies.start(mixed, mixed_hbm)]
+    last.wait()
+    rotated[...] = product(left[...], mixed[...], TN)
+    outputs.append(copies.start(rotated, upper_hbm))
+    for copy in outputs:
+        copy.wait()
+
+
+def rotate_step(place, own, other_first, own_pieces, other_pieces):
+    order, half = other_first.shape
+    count = len(own_pieces)
+    shape, vmem = jax.ShapeDtypeStruct, pltpu.VMEM
+    bf16, f32 = jnp.bfloat16, jnp.float32
+    columns = vmem((order, half), bf16)
+    return kernel_call(
+        functools.partial(rotate_kernel, count),
+        "rotate_step",
+        (shape((order, half), bf16), shape((half, half), f32)),
+        [
+            columns,
+            columns,
+            vmem((order, order), bf16),
+            columns,
+            vmem((half, half), f32),
+            pltpu.SemaphoreType.DMA((2 * count + 4,)),
+        ],
+        2 * order * order * half + 2 * order * half * half,
+        (place, *own, other_first, *own_pieces, *other_pieces),
+    )
+
+
+def moment_kernel(place_ref, *refs):
+    own, other, (mixed_hbm, upper_hbm, moments_hbm, first_hbm, second_hbm) = refs[:2], refs[2:4], refs[4:9]
+    near_hbm, far_hbm, first_out, second_out = refs[9:13]
+    left, left_rows, right, moments, first_rows, second_rows, mixed, rotated, normal, near, far, semaphores = refs[13:]
     row_count, half_width = first_rows.shape
     order = left.shape[0]
     f32, bf16 = jnp.float32, jnp.bfloat16
     first = place_ref[0] == 0
-    here = rows_from(place_ref[1], 0, row_count, count)
+    here = rows_from(place_ref[1], 0, row_count, order // row_count)
     upper, lower = pl.ds(0, half_width), pl.ds(half_width, half_width)
     copies = Copies(semaphores)
-    early = [copies.start_either(first, other[0], own[1], right)]
-    for k in range(count):
-        span = rows_from(place_ref[1], k, row_count, count)
-        early.append(copies.start_either(first, own_pieces[k], other_pieces[k], block.at[span, upper]))
-        early.append(copies.start_either(first, other_pieces[k], own_pieces[k], block.at[span, lower]))
+    waits = [
+        copies.start(moments_hbm, moments),
+        copies.start(upper_hbm, rotated.at[upper, :]),
+        copies.start_either(first, own[0].at[here, :], other[0].at[here, :], left_rows.at[:, upper]),
+        copies.start_either(first, own[1].at[here, :], other[1].at[here, :], left_rows.at[:, lower]),
+    ]
     late = [
-        copies.start_either(first, own[0], other[0], left.at[:, upper]),
-        copies.start_either(first, own[1], other[1], left.at[:, lower]),
-        copies.start(moments_hbm, moments),
+        copies.start(mixed_hbm, mixed),
+        copies.start_either(first, own[1], other[1], left),
         copies.start(first_hbm, first_rows),
         copies.start(second_hbm, second_rows),
+        copies.start_either(first, other[0], own[1], right),
     ]
-    for copy in early:
-        copy.wait()
-    mixed[...] = product(block[...], right[...], NN).astype(bf16)
-    for copy in late:
-        copy.wait()
-    total = jnp.zeros(weighted.shape, f32)
+    for copy in waits:
+        copy.wait()
+    total = jnp.zeros(near.shape, f32)
     width = order // 4
     for start in range(0, order, width):
         span = slice(start, start + width)
-        turn = product(left[:, span], mixed[...], TN)
-        rotated[span, :] = turn
+        if start == half_width:
+            for copy in late:
+                copy.wait()
+        if start >= half_width:
+            rotated[span, :] = product(left[:, start - half_width : start - half_width + width], mixed[...], TN)
+        turn = rotated[span, :]
         new_first = 0.95 * moments[span, :half_width].astype(f32) + 0.05 * turn
         new_second = 0.95 * moments[span, half_width:].astype(f32) + 0.05 * turn * turn
         normal[span, :] = (new_first / (jnp.sqrt(new_second) + 1e-08)).astype(bf16)
-        total = total + product(left[here, span], normal[span, :], NN)
-    weighted[...] = total.astype(bf16)
-    outputs = [copies.start(weighted, weighted_hbm)]
+        total = total + product(left_rows[:, span], normal[span, :], NN)
+    part = product(total.astype(bf16), right[...], NT)
+
+    @pl.when(first)
+    def _():
+        near[...] = part[:, :half_width]
+        far[...] = part[:, half_width:].astype(bf16)
+
+    @pl.when(jnp.logical_not(first))
+    def _():
+        near[...] = part[:, half_width:]
+        far[...] = part[:, :half_width].astype(bf16)
+
+    outputs = [copies.start(far, far_hbm), copies.start(near, near_hbm)]
     turn = rotated[here, :]
     first_rows[...] = 0.95 * first_rows[...] + 0.05 * turn
     second_rows[...] = 0.95 * second_rows[...] + 0.05 * turn * turn
@@ -431,64 +488,31 @@
         copy.wait()
 
 
-def moment_step(place, own, other, own_pieces, other_pieces, moments, first, second):
+def moment_step(place, own, other, mixed, upper, moments, first, second):
     order = own[0].shape[0]
     half = first.shape[1]
-    count = len(own_pieces)
     f32, bf16 = jnp.float32, jnp.bfloat16
     shape, vmem = jax.ShapeDtypeStruct, pltpu.VMEM
     return kernel_call(
-        functools.partial(moment_kernel, count),
+        moment_kernel,
         "moment_step",
-        (shape(first.shape, bf16), shape(first.shape, f32), shape(first.shape, f32)),
+        (shape(first.shape, f32), shape(first.shape, bf16), shape(first.shape, f32), shape(first.shape, f32)),
         [
-            vmem((order, order), bf16),
-            vmem((order, half), bf16),
-            vmem((order, order), bf16),
+            vmem((order, half), bf16),
+            vmem((first.shape[0], order), bf16),
+            vmem((order, half), bf16),
             vmem((order, order), bf16),
             vmem(first.shape, f32),
             vmem(first.shape, f32),
             vmem((order, half), bf16),
             vmem((order, half), f32),
             vmem((order, half), bf16),
+            vmem(first.shape, f32),
             vmem(first.shape, bf16),
-            pltpu.SemaphoreType.DMA((2 * count + 9,)),
+            pltpu.SemaphoreType.DMA((13,)),
         ],
-        4 * order * order * half,
-        (place, *own, *other, *own_pieces, *other_pieces, moments, first, second),
-    )
-
-
-def direction_kernel(place_ref, *refs):
-    own, other, (mine_hbm, theirs_hbm, out_hbm) = refs[:2], refs[2:4], refs[4:7]
-    near, far, mine, theirs, out, semaphores = refs[7:]
-    half = near.shape[0]
-    upper, lower = pl.ds(0, half), pl.ds(half, half)
-    first = place_ref[0] == 0
-    copies = Copies(semaphores)
-    waits = [
-        copies.start(mine_hbm, mine),
-        copies.start(theirs_hbm, theirs),
-        copies.start_either(first, other[0].at[upper, :], own[1].at[lower, :], near),
-        copies.start_either(first, other[1].at[upper, :], own[0].at[lower, :], far),
-    ]
-    for copy in waits:
-        copy.wait()
-    out[...] = (product(mine[...], near[...], NT) + product(theirs[...], far[...], NT)).astype(out.dtype)
-    copies.start(out, out_hbm).wait()
-
-
-def direction_step(place, own, other, mine, theirs):
-    half = mine.shape[1]
-    vmem = pltpu.VMEM
-    square, rows = vmem((half, half), mine.dtype), vmem(mine.shape, mine.dtype)
-    return kernel_call(
-        direction_kernel,
-        "direction_step",
-        jax.ShapeDtypeStruct(mine.shape, mine.dtype),
-        [square, square, rows, rows, rows, pltpu.SemaphoreType.DMA((5,))],
-        4 * mine.shape[0] * half * half,
-        (place, *own, *other, mine, theirs),
+        2 * order * half * half,
+        (place, *own, *other, mixed, upper, moments, first, second),
     )
 
 
@@ -578,10 +602,11 @@
     first_other = sibling(first_q)
     second_q, new_rows = second_half(place, late, factor_whole, first_q, row_count)
     own, other = (first_q, second_q), (first_other, sibling(second_q))
-    weighted, first_new, second_new = moment_step(
-        place, own, other, own_pieces, other_pieces, moments, first_moment[0], second_moment[0]
+    mixed, upper = rotate_step(place, own, first_other, own_pieces, other_pieces)
+    near, far, first_new, second_new = moment_step(
+        place, own, other, mixed, upper, moments, first_moment[0], second_moment[0]
     )
-    direction = direction_step(place, own, other, weighted, sibling(weighted))
+    direction = (near + sibling(far).astype(jnp.float32)).astype(bf16)
     return (new_factor_rows[None], new_rows[None], first_new[None], second_new[None], direction[None])
 
 

time: 169 us -> 166 us (0.982)
  waiting for transfers between devices: 54.3 us -> 47.7 us
  other arithmetic: 2.55 us -> 4.37 us
    all_gather x1, waiting for transfers between devices: 3.91 us -> 0.02 us  [body(): moments = lax.all_gather(moments, 'fsdp', axis=0, tiled=True)]
    ppermute x10, waiting for transfers between devices: 16.8 us -> 14.2 us  [exchanged(): return lax.ppermute(block, axis, [(i, partner_of(i)) for i in range(count)])]
    broadcast_in_dim x0 -> x1, other arithmetic: none -> 1.82 us  [body(): direction[None]]
  transfers between devices with their start and end apart: 19 -> 19, of which waited for: 12 -> 10; matrix products, arithmetic and copies ran while one was open for 1% -> 1% of each run, Pallas kernels for 34% -> 38%
where the time goes in v4:
time: 166 us; the launch traced here: 164 us
  Pallas kernels  72.5 us (44%)
  waiting for transfers between devices  47.7 us (29%)
  starting transfers between devices  22.3 us (13%)
  between operations  14 us (8%)
  other arithmetic  4.37 us (3%)
  local copies, waits for them, and re-layouts  2.69 us (2%)
    pallas_call x4, Pallas kernels, kernel_call(): pl.pallas_call(kernel, out_shape=out_shape, in_specs=[SMEM] + [HBM] * (le...  70 us
    ppermute x6, waiting for transfers between devices, pieces_by_distance(): lax.ppermute(shard, axis, [(i, (i + distance) % count) for i in range(cou...  33.5 us
    ppermute x10, starting transfers between devices, exchanged(): return lax.ppermute(block, axis, [(i, partner_of(i)) for i in range(count)])  16.9 us
    ppermute x10, waiting for transfers between devices, exchanged(): return lax.ppermute(block, axis, [(i, partner_of(i)) for i in range(count)])  14.2 us
    ppermute x6, starting transfers between devices, pieces_by_distance(): lax.ppermute(shard, axis, [(i, (i + distance) % count) for i in range(cou...  5.34 us
  transfers between devices with their start and end apart: 19, of which 10 were waited for; matrix products, arithmetic and copies ran while one was open for 1% of the time, Pallas kernels for 38%

profile of v4, /device:TPU:13, one launch (start us, length us, event | category | flops | bytes accessed | tf_op | source)
XLA Modules:
  0.0 163.7 jit_solution(6945298290267067599)
XLA Ops:
  7.9 2.6 %gather_shares.1 = (bf16[256,256]{1,0:T(8,128)(2,1)}, bf16[256,896]{1,0:T(8,128)(2,1)}, bf16[256,512]{1,0:T(8,128)(2,1)}) custom-call(s32[2]{0:T(128)} %pad_add_fusion.place_ref, f32[256,1024]{1,0:T(8,128)} %bitcast.21, f32[256,1024]{1,0:T(8,128)} %bitcast.20), custom_call_target="tpu_custom_call" | custom-call | bytes 3145728 | tf_op jit(solution)/shard_map/gather_shares/pallas_call | solution.py:235
  11.6 1.4 collective-permute-start.1
  13.0 1.0 collective-permute-start.2
  14.0 1.5 collective-permute-start.3
  16.0 12.4 %collective-permute-done.2.refs_10_ = bf16[256,256]{1,0:T(8,128)(2,1)S(1)} collective-permute-done((bf16[256,256]{1,0:T(8,128)(2,1)S(1)}, bf16[256,256]{1,0:T(8,128)(2,1)S(1)}, u32[]{:S(2)}, u32[]{:S(2)}) %collective-permute-start.2) | collective-permute-done | bytes 131104 | tf_op jit(solution)/shard_map/ppermute | solution.py:573
  28.3 7.8 %collective-permute-done.3.refs_11_ = bf16[256,256]{1,0:T(8,128)(2,1)} collective-permute-done((bf16[256,256]{1,0:T(8,128)(2,1)S(1)}, bf16[256,256]{1,0:T(8,128)(2,1)}, u32[]{:S(2)}, u32[]{:S(2)}) %collective-permute-start.3) | collective-permute-done | bytes 131104 | tf_op jit(solution)/shard_map/ppermute | solution.py:573
  36.2 1.2 collective-permute-start.4
  37.5 7.1 %collective-permute-done.4 = bf16[2,256,512]{2,1,0:T(8,128)(2,1)S(1)} collective-permute-done((bf16[2,256,512]{2,1,0:T(8,128)(2,1)S(1)}, bf16[2,256,512]{2,1,0:T(8,128)(2,1)S(1)}, u32[]{:S(2)}, u32[]{:S(2)}) %collective-permute-start.4) | collective-permute-done | bytes 524320 | tf_op jit(solution)/shard_map/ppermute | solution.py:521
  46.1 4.5 %collective-permute-done.5 = bf16[1,256,512]{2,1,0:T(8,128)(2,1)S(1)} collective-permute-done((bf16[1,256,512]{2,1,0:T(8,128)(2,1)S(1)}, bf16[1,256,512]{2,1,0:T(8,128)(2,1)S(1)}, u32[]{:S(2)}, u32[]{:S(2)}) %collective-permute-start.5) | collective-permute-done | bytes 262176 | tf_op jit(solution)/shard_map/ppermute | solution.py:521
  50.8 1.4 collective-permute-start.8
  52.2 8.7 %collective-permute-start.9 = (bf16[256,512]{1,0:T(8,128)(2,1)S(1)}, bf16[256,512]{1,0:T(8,128)(2,1)S(1)}, u32[]{:S(2)}, u32[]{:S(2)}) collective-permute-start(bf16[256,512]{1,0:T(8,128)(2,1)S(1)} %fusion.refs_0_), channel_id=1, source_target_pairs={{0,4},{4,0},{8,12},{12,8},{16,20},{20,16},{24,28},{28,24},{1,5},{5... | collective-permute-start | bytes 786440 | tf_op jit(solution)/shard_map/ppermute | solution.py:521
  60.9 9.2 %collective-permute-done.6.refs_1_ = bf16[256,512]{1,0:T(8,128)(2,1)S(1)} collective-permute-done((bf16[256,512]{1,0:T(8,128)(2,1)S(1)}, bf16[256,512]{1,0:T(8,128)(2,1)S(1)}, u32[]{:S(2)}, u32[]{:S(2)}) %collective-permute-start.6) | collective-permute-done | bytes 262176 | tf_op jit(solution)/shard_map/ppermute | solution.py:573
  70.1 2.6 %collective-permute-start.10 = (bf16[256,512]{1,0:T(8,128)(2,1)S(1)}, bf16[256,512]{1,0:T(8,128)(2,1)S(1)}, u32[]{:S(2)}, u32[]{:S(2)}) collective-permute-start(bf16[256,512]{1,0:T(8,128)(2,1)S(1)} %collective-permute-done.6.refs_1_), channel_id=1, source_target_pairs={{0,4},{4,0},{8,12},{12,8},{16,20},{20,16},{24,28},{28,24},{1,5},{5... | collective-permute-start | bytes 786440 | tf_op jit(solution)/shard_map/ppermute | solution.py:521
  72.7 3.1 %collective-permute-done.7.refs_2_ = bf16[256,512]{1,0:T(8,128)(2,1)S(1)} collective-permute-done((bf16[256,512]{1,0:T(8,128)(2,1)S(1)}, bf16[256,512]{1,0:T(8,128)(2,1)S(1)}, u32[]{:S(2)}, u32[]{:S(2)}) %collective-permute-start.7) | collective-permute-done | bytes 262176 | tf_op jit(solution)/shard_map/ppermute | solution.py:573
  75.8 1.5 collective-permute-start.11
  79.0 1.1 collective-permute-done.12.refs_7_
  80.8 29.7 %first_half.1 = (bf16[1024,1024]{1,0:T(8,128)(2,1)}, f32[256,1024]{1,0:T(8,128)}, bf16[1024,512]{1,0:T(8,128)(2,1)}) custom-call(s32[2]{0:T(128)} %pad_add_fusion.place_ref, bf16[1024,896]{1,0:T(8,128)(2,1)} %all-gather.4.cloned.1.call-done.gathered_hbm, f32[256,1024]{1,0:T(8,128)} %bitcast.22, bf16[256,512]{1,0:T(8,128)(2,1)} %copy-done.5, ...), custom_call_target="tpu_custom_call" | custom-call | flops 6442450944 | bytes 16777216 | tf_op jit(solution)/shard_map/first_half/pallas_call | solution.py:143
  111.0 27.3 %second_half.1 = (bf16[1024,512]{1,0:T(8,128)(2,1)}, bf16[256,1024]{1,0:T(8,128)(2,1)}) custom-call(s32[2]{0:T(128)} %pad_add_fusion.place_ref, bf16[1024,512]{1,0:T(8,128)(2,1)} %all-gather.6.cloned.1.call-done.columns_hbm, bf16[1024,1024]{1,0:T(8,128)(2,1)} %get-tuple-element.36.whole_hbm, bf16[1024,512]{1,0:T(8,128)(2,1)} %get-tuple-element.37.before_hbm.own_first.refs_0_), custom_call_target="tpu_custom_call" | custom-call | flops 4294967296 | bytes 16777216 | tf_op jit(solution)/shard_map/second_half/pallas_call | solution.py:143
  138.6 1.0 copy-done.3
  139.5 5.6 %rotate_step.1 = (bf16[1024,512]{1,0:T(8,128)(2,1)}, f32[512,512]{1,0:T(8,128)}) custom-call(s32[2]{0:T(128)} %pad_add_fusion.place_ref, bf16[1024,512]{1,0:T(8,128)(2,1)} %get-tuple-element.37.before_hbm.own_first.refs_0_, bf16[1024,512]{1,0:T(8,128)(2,1)} %get-tuple-element.39.own_second.refs_1_, bf16[1024,512]{1,0:T(8,128)(2,1)} %copy-done.3, ...), custom_call_target="tpu_custom_call" | custom-call | flops 1610612736 | bytes 16777216 | tf_op jit(solution)/shard_map/rotate_step/pallas_call | solution.py:143
  145.2 1.0 copy-done.4
  146.2 7.3 %moment_step.1 = (f32[256,512]{1,0:T(8,128)}, bf16[256,512]{1,0:T(8,128)(2,1)}, f32[256,512]{1,0:T(8,128)}, f32[256,512]{1,0:T(8,128)}) custom-call(s32[2]{0:T(128)} %pad_add_fusion.place_ref, bf16[1024,512]{1,0:T(8,128)(2,1)} %get-tuple-element.37.before_hbm.own_first.refs_0_, bf16[1024,512]{1,0:T(8,128)(2,1)} %get-tuple-element.39.own_second.refs_1_, ...), custom_call_target="tpu_custom_call" | custom-call | flops 536870912 | bytes 16777216 | tf_op jit(solution)/shard_map/moment_step/pallas_call | solution.py:143
  153.9 1.4 collective-permute-done.15
  155.3 1.8 %fusion.1 = bf16[1,256,512]{2,1,0:T(8,128)(2,1)} fusion(f32[256,512]{1,0:T(8,128)} %get-tuple-element.45, bf16[256,512]{1,0:T(8,128)(2,1)S(1)} %collective-permute-done.15), kind=kLoop, calls=%fused_computation.8 | loop fusion | flops 393216 | bytes 1048576 | tf_op jit(solution)/shard_map/broadcast_in_dim | solution.py:610
  (65 shorter events, 7.4 us)
Async XLA Ops:
  7.2 72.9 %all-gather.4.cloned.1.call-start = ((), (), s32[]{:S(2)}) async-start(), calls=%async_computation | async-start | bytes 2293760 | tf_op jit(solution)/shard_map/all_gather | solution.py:588
  10.5 100.6 %all-gather.6.cloned.1.call-start = ((), (), s32[]{:S(2)}) async-start(), calls=%async_computation.1 | async-start | bytes 1310720 | tf_op jit(solution)/shard_map/all_gather | solution.py:589
  10.9 4.6 %collective-permute-start = (bf16[4,256,512]{2,1,0:T(8,128)(2,1)S(1)}, bf16[4,256,512]{2,1,0:T(8,128)(2,1)S(1)}, u32[]{:S(2)}, u32[]{:S(2)}) collective-permute-start(bf16[4,256,512]{2,1,0:T(8,128)(2,1)S(1)} %pad_maximum_fusion), channel_id=1, source_target_pairs={{0,4},{4,0},{8,12},{12,8},{16,20},{20,16},{24,28},{28,24},{1,5},{5... | collective-permute-start | bytes 3145736 | tf_op jit(solution)/shard_map/ppermute | solution.py:521
  11.6 4.4 %collective-permute-start.1 = (bf16[256,256]{1,0:T(8,128)(2,1)S(1)}, bf16[256,256]{1,0:T(8,128)(2,1)S(1)}, u32[]{:S(2)}, u32[]{:S(2)}) collective-permute-start(bf16[256,256]{1,0:T(8,128)(2,1)S(1)} %copy-done.13), channel_id=1, source_target_pairs={{0,1},{1,2},{2,3},{3,0},{4,5},{5,6},{6,7},{7,4},{8,9},{9,10},{10,1... | collective-permute-start | bytes 393224 | tf_op jit(solution)/shard_map/ppermute | solution.py:573
  13.0 15.4 %collective-permute-start.2 = (bf16[256,256]{1,0:T(8,128)(2,1)S(1)}, bf16[256,256]{1,0:T(8,128)(2,1)S(1)}, u32[]{:S(2)}, u32[]{:S(2)}) collective-permute-start(bf16[256,256]{1,0:T(8,128)(2,1)S(1)} %copy-done.13), channel_id=1, source_target_pairs={{0,2},{1,3},{2,0},{3,1},{4,6},{5,7},{6,4},{7,5},{8,10},{9,11},{10,... | collective-permute-start | bytes 393224 | tf_op jit(solution)/shard_map/ppermute | solution.py:573
  14.0 22.2 %collective-permute-start.3 = (bf16[256,256]{1,0:T(8,128)(2,1)S(1)}, bf16[256,256]{1,0:T(8,128)(2,1)}, u32[]{:S(2)}, u32[]{:S(2)}) collective-permute-start(bf16[256,256]{1,0:T(8,128)(2,1)S(1)} %copy-done.13), channel_id=1, source_target_pairs={{0,3},{1,0},{2,1},{3,2},{4,7},{5,4},{6,5},{7,6},{8,11},{9,8},{10,9... | collective-permute-start | bytes 393224 | tf_op jit(solution)/shard_map/ppermute | solution.py:573
  15.7 29.4 %copy-start = (f32[1,256,512]{2,1,0:T(8,128)S(1)}, f32[1,256,512]{2,1,0:T(8,128)}, u32[]{:S(2)}) copy-start(f32[1,256,512]{2,1,0:T(8,128)} %param.9) | copy-start | bytes 1572868
  15.8 29.3 %copy-start.1 = (f32[1,256,512]{2,1,0:T(8,128)S(1)}, f32[1,256,512]{2,1,0:T(8,128)}, u32[]{:S(2)}) copy-start(f32[1,256,512]{2,1,0:T(8,128)} %param.8) | copy-start | bytes 1572868
  16.0 29.2 %copy-start.14 = (bf16[256,256]{1,0:T(8,128)(2,1)}, bf16[256,256]{1,0:T(8,128)(2,1)S(1)}, u32[]{:S(2)}) copy-start(bf16[256,256]{1,0:T(8,128)(2,1)S(1)} %collective-permute-done.1.refs_9_) | copy-start | bytes 393220
  28.3 16.8 %copy-start.15 = (bf16[256,256]{1,0:T(8,128)(2,1)}, bf16[256,256]{1,0:T(8,128)(2,1)S(1)}, u32[]{:S(2)}) copy-start(bf16[256,256]{1,0:T(8,128)(2,1)S(1)} %collective-permute-done.2.refs_10_) | copy-start | bytes 393220
  36.2 8.4 %collective-permute-start.4 = (bf16[2,256,512]{2,1,0:T(8,128)(2,1)S(1)}, bf16[2,256,512]{2,1,0:T(8,128)(2,1)S(1)}, u32[]{:S(2)}, u32[]{:S(2)}) collective-permute-start(bf16[2,256,512]{2,1,0:T(8,128)(2,1)S(1)} %broadcast_select_fusion), channel_id=1, source_target_pairs={{0,16},{4,12},{8,24},{12,4},{16,0},{20,28},{24,8},{28,20},{1,17},{... | collective-permute-start | bytes 1572872 | tf_op jit(solution)/shard_map/ppermute | solution.py:521
  37.4 107.8 %all-gather.8.cloned.1.call-start = ((), (), s32[]{:S(2)}) async-start(), calls=%async_computation.2 | async-start | bytes 2621440 | tf_op jit(solution)/shard_map/all_gather | solution.py:595
  44.9 5.7 %collective-permute-start.5 = (bf16[1,256,512]{2,1,0:T(8,128)(2,1)S(1)}, bf16[1,256,512]{2,1,0:T(8,128)(2,1)S(1)}, u32[]{:S(2)}, u32[]{:S(2)}) collective-permute-start(bf16[1,256,512]{2,1,0:T(8,128)(2,1)S(1)} %broadcast_select_fusion.9), channel_id=1, source_target_pairs={{0,8},{4,20},{8,0},{12,28},{16,24},{20,4},{24,16},{28,12},{1,9},{5... | collective-permute-start | bytes 786440 | tf_op jit(solution)/shard_map/ppermute | solution.py:521
  50.7 29.5 %copy-start.5 = (bf16[256,512]{1,0:T(8,128)(2,1)}, bf16[256,512]{1,0:T(8,128)(2,1)S(1)}, u32[]{:S(2)}) copy-start(bf16[256,512]{1,0:T(8,128)(2,1)S(1)} %fusion.refs_0_) | copy-start | bytes 786436
  50.7 19.4 %collective-permute-start.6 = (bf16[256,512]{1,0:T(8,128)(2,1)S(1)}, bf16[256,512]{1,0:T(8,128)(2,1)S(1)}, u32[]{:S(2)}, u32[]{:S(2)}) collective-permute-start(bf16[256,512]{1,0:T(8,128)(2,1)S(1)} %fusion.refs_0_), channel_id=1, source_target_pairs={{0,1},{1,2},{2,3},{3,0},{4,5},{5,6},{6,7},{7,4},{8,9},{9,10},{10,1... | collective-permute-start | bytes 786440 | tf_op jit(solution)/shard_map/ppermute | solution.py:573
  50.8 25.1 %collective-permute-start.7 = (bf16[256,512]{1,0:T(8,128)(2,1)S(1)}, bf16[256,512]{1,0:T(8,128)(2,1)S(1)}, u32[]{:S(2)}, u32[]{:S(2)}) collective-permute-start(bf16[256,512]{1,0:T(8,128)(2,1)S(1)} %fusion.refs_0_), channel_id=1, source_target_pairs={{0,2},{1,3},{2,0},{3,1},{4,6},{5,7},{6,4},{7,5},{8,10},{9,11},{10,... | collective-permute-start | bytes 786440 | tf_op jit(solution)/shard_map/ppermute | solution.py:573
  50.8 27.3 %collective-permute-start.8 = (bf16[256,512]{1,0:T(8,128)(2,1)S(1)}, bf16[256,512]{1,0:T(8,128)(2,1)S(1)}, u32[]{:S(2)}, u32[]{:S(2)}) collective-permute-start(bf16[256,512]{1,0:T(8,128)(2,1)S(1)} %fusion.refs_0_), channel_id=1, source_target_pairs={{0,3},{1,0},{2,1},{3,2},{4,7},{5,4},{6,5},{7,6},{8,11},{9,8},{10,9... | collective-permute-start | bytes 786440 | tf_op jit(solution)/shard_map/ppermute | solution.py:573
  52.2 26.7 %collective-permute-start.9 = (bf16[256,512]{1,0:T(8,128)(2,1)S(1)}, bf16[256,512]{1,0:T(8,128)(2,1)S(1)}, u32[]{:S(2)}, u32[]{:S(2)}) collective-permute-start(bf16[256,512]{1,0:T(8,128)(2,1)S(1)} %fusion.refs_0_), channel_id=1, source_target_pairs={{0,4},{4,0},{8,12},{12,8},{16,20},{20,16},{24,28},{28,24},{1,5},{5... | collective-permute-start | bytes 786440 | tf_op jit(solution)/shard_map/ppermute | solution.py:521
  70.1 8.9 %collective-permute-start.10 = (bf16[256,512]{1,0:T(8,128)(2,1)S(1)}, bf16[256,512]{1,0:T(8,128)(2,1)S(1)}, u32[]{:S(2)}, u32[]{:S(2)}) collective-permute-start(bf16[256,512]{1,0:T(8,128)(2,1)S(1)} %collective-permute-done.6.refs_1_), channel_id=1, source_target_pairs={{0,4},{4,0},{8,12},{12,8},{16,20},{20,16},{24,28},{28,24},{1,5},{5... | collective-permute-start | bytes 786440 | tf_op jit(solution)/shard_map/ppermute | solution.py:521
  75.8 3.2 %collective-permute-start.11 = (bf16[256,512]{1,0:T(8,128)(2,1)S(1)}, bf16[256,512]{1,0:T(8,128)(2,1)S(1)}, u32[]{:S(2)}, u32[]{:S(2)}) collective-permute-start(bf16[256,512]{1,0:T(8,128)(2,1)S(1)} %collective-permute-done.7.refs_2_), channel_id=1, source_target_pairs={{0,4},{4,0},{8,12},{12,8},{16,20},{20,16},{24,28},{28,24},{1,5},{5... | collective-permute-start | bytes 786440 | tf_op jit(solution)/shard_map/ppermute | solution.py:521
  78.1 2.0 %collective-permute-start.12 = (bf16[256,512]{1,0:T(8,128)(2,1)S(1)}, bf16[256,512]{1,0:T(8,128)(2,1)S(1)}, u32[]{:S(2)}, u32[]{:S(2)}) collective-permute-start(bf16[256,512]{1,0:T(8,128)(2,1)S(1)} %collective-permute-done.8.refs_3_), channel_id=1, source_target_pairs={{0,4},{4,0},{8,12},{12,8},{16,20},{20,16},{24,28},{28,24},{1,5},{5... | collective-permute-start | bytes 786440 | tf_op jit(solution)/shard_map/ppermute | solution.py:521
  110.6 28.0 %collective-permute-start.13 = (bf16[1024,512]{1,0:T(8,128)(2,1)}, bf16[1024,512]{1,0:T(8,128)(2,1)S(1)}, u32[]{:S(2)}, u32[]{:S(2)}) collective-permute-start(bf16[1024,512]{1,0:T(8,128)(2,1)} %get-tuple-element.37.before_hbm.own_first.refs_0_), channel_id=1, source_target_pairs={{0,4},{4,0},{8,12},{12,8},{16,20},{20,16},{24,28},{28,24},{1,5},{5... | collective-permute-start | bytes 3145736 | tf_op jit(solution)/shard_map/ppermute | solution.py:521
  138.4 6.8 %collective-permute-start.14 = (bf16[1024,512]{1,0:T(8,128)(2,1)}, bf16[1024,512]{1,0:T(8,128)(2,1)S(1)}, u32[]{:S(2)}, u32[]{:S(2)}) collective-permute-start(bf16[1024,512]{1,0:T(8,128)(2,1)} %get-tuple-element.39.own_second.refs_1_), channel_id=1, source_target_pairs={{0,4},{4,0},{8,12},{12,8},{16,20},{20,16},{24,28},{28,24},{1,5},{5... | collective-permute-start | bytes 3145736 | tf_op jit(solution)/shard_map/ppermute | solution.py:521
  153.5 1.8 %collective-permute-start.15 = (bf16[256,512]{1,0:T(8,128)(2,1)}, bf16[256,512]{1,0:T(8,128)(2,1)S(1)}, u32[]{:S(2)}, u32[]{:S(2)}) collective-permute-start(bf16[256,512]{1,0:T(8,128)(2,1)} %get-tuple-element.46), channel_id=1, source_target_pairs={{0,4},{4,0},{8,12},{12,8},{16,20},{20,16},{24,28},{28,24},{1,5},{5... | collective-permute-start | bytes 786440 | tf_op jit(solution)/shard_map/ppermute | solution.py:521
  (11 other events, 27.0 us)
Sparse Core Ops, SparseCore 0:
  10.6 45.3 all-gather.3
  58.1 40.4 all-gather.5
  100.8 44.3 all-gather.7
